TPU v7x, 256 devices: a whole 4x4x8 slice. The times are simulated.
256 devices in a mesh: blk: 128 (over z, x_lo, y, core), rep: 2 (over x_hi).
Axes of the slice: x: 4 (x_hi: 2, x_lo: 2; x = x_hi * 2 + x_lo), y: 4, z: 8, core: 2. Of those that a mesh axis runs over, the one named last changes fastest.
Arguments:
- saved_rows: float32 [131072, 400], P('blk'), may hold values from -1.8 to 1.8
- saved_state: float32 [131072], P('blk'), may hold values from 0.001 to 0.1
- old_starts: int32 [64], replicated, may hold values from 0 to 121087, as said below
- new_starts: int32 [128], replicated, may hold values from 0 to 121920, as said below
- relations: float32 [4131, 400], replicated, may hold values from -3.6 to 3.6
- source_rows: int32 [128, 4, 2, 1000], P('blk'), may hold values from 0 to 896
- target_rows: int32 [128, 4, 2, 1000], P('blk'), may hold values from 0 to 896
- relation_ids: int32 [128, 4, 2, 1000], P('blk'), may hold values from 0 to 4130
- negative_rows: int32 [128, 4, 2, 512], P('blk'), may hold values from 0 to 896
- live_groups: int32 [128, 4], P('blk'), may hold values from 1 to 2
Outputs:
- embeddings: float32 [131072, 400], P(('blk', 'rep'))
- adagrad_state: float32 [131072], P(('blk', 'rep'))
Inputs may be any that keep to these rules, and one draw needn't show every extreme that they name: new_starts[q] = q * 960 + an offset of 0 to 63, and 0 for q = 0 and for the last q; where q * 64 is a multiple of 128, the offset is smaller than the offset of saved partition q * 64 / 128; the last partition ends at entity 122880. old_starts[p] = p * 1920 + an offset of 1 to 127; the offset of partition 0 is 0 and that of the last is 127; the last saved partition ends at entity 122880.
All inputs are finite; a program needn't handle non-finite values.
Results may differ from a plain program's by a relative error of at most 0.00031.
Values sent between devices are 32-bit elements; how exact they have to be, the bound alone decides.
A program may use at most 128 MiB of HBM per device.

v0:
```python
import jax
import jax.numpy as jnp
from jax import lax
from jax.sharding import PartitionSpec as P

LR_RATE = 0.2
EPSILON = 1e-10


def shifted(value, axis, steps):
    count = lax.axis_size(axis)
    initial, last = (max(0, -steps), min(count, count - steps))
    return lax.ppermute(value, axis, [(source, source + steps) for source in range(initial, last)])


def partner(value, axis, distance):
    mask = 2**distance
    pairs = [(source, source ^ mask) for source in range(lax.axis_size(axis))]
    return lax.ppermute(value, axis, pairs)


def from_behind(block, axis, distance):
    devices = range(lax.axis_size(axis))
    route = [((i - distance) % len(devices), i) for i in devices]
    return lax.ppermute(block, axis, route)


def group_grads(left_table, right_table, relations, sources, targets, rel_index, negatives):
    half_width = left_table.shape[1] // 2
    src_emb = jnp.take(left_table, sources, axis=0)
    dst_emb = jnp.take(right_table, targets, axis=0)
    rel_emb = jnp.take(relations, rel_index, axis=0)
    neg_emb = jnp.take(right_table, negatives, axis=0)
    s_re, s_im = (src_emb[:, :half_width], src_emb[:, half_width:])
    r_re, r_im = (rel_emb[:, :half_width], rel_emb[:, half_width:])
    query = jnp.concatenate([s_re * r_re - s_im * r_im, s_re * r_im + s_im * r_re], axis=1)
    positive = jnp.sum(query * dst_emb, axis=1)
    query_b = query.astype(jnp.bfloat16)
    neg_b = neg_emb.astype(jnp.bfloat16)
    scores = lax.dot_general(
        query_b, neg_b, (((1,), (1,)), ((), ())), preferred_element_type=jnp.float32
    )
    dpos = -jax.nn.sigmoid(-positive)
    dneg = (jax.nn.sigmoid(scores) / negatives.shape[0]).astype(jnp.bfloat16)
    grad_query = dpos[:, None] * dst_emb + jnp.dot(dneg, neg_b, preferred_element_type=jnp.float32)
    grad_neg = lax.dot_general(
        dneg, query_b, (((0,), (0,)), ((), ())), preferred_element_type=jnp.float32
    )
    grad_dst = dpos[:, None] * query
    gq_re, gq_im = (grad_query[:, :half_width], grad_query[:, half_width:])
    grad_src = jnp.concatenate([gq_re * r_re + gq_im * r_im, gq_im * r_re - gq_re * r_im], axis=1)
    left_grad = jnp.zeros(left_table.shape, jnp.float32).at[sources].add(grad_src)
    right_grad = (
        jnp.zeros(right_table.shape, jnp.float32)
        .at[targets]
        .add(grad_dst)
        .at[negatives]
        .add(grad_neg)
    )
    return (left_grad, right_grad)


def restore_slots(old_starts, new_starts, slot_count, blocks):
    position = lax.axis_index("blk")
    entities = blocks * (slot_count - slot_count // 16)
    old_cap = slot_count * blocks // old_starts.shape[0]
    first = lax.dynamic_index_in_dim(new_starts, position, 0, keepdims=False)
    following = lax.dynamic_index_in_dim(
        new_starts, jnp.minimum(position + 1, blocks - 1), 0, keepdims=False
    )
    last_id = jnp.where(position + 1 < blocks, following, entities)
    slot_ids = jnp.arange(slot_count, dtype=jnp.int32)
    entity_ids = first + slot_ids
    valid = slot_ids < last_id - first
    partition = jnp.sum((old_starts[None, :] <= entity_ids[:, None]).astype(jnp.int32), axis=1) - 1
    partition = jnp.clip(partition, 0, old_starts.shape[0] - 1)
    source_slot = partition * old_cap + entity_ids - jnp.take(old_starts, partition)
    source_slot = jnp.where(valid, source_slot, 0)
    return (source_slot, valid, position)


def local(
    saved_rows,
    saved_state,
    old_starts,
    new_starts,
    relations,
    source_rows,
    target_rows,
    relation_ids,
    negative_rows,
    live_groups,
):
    slot_count = saved_rows.shape[0]
    blocks = lax.axis_size("blk")
    source_slot, valid, position = restore_slots(old_starts, new_starts, slot_count, blocks)
    lower_rows, lower_state = shifted((saved_rows, saved_state), "blk", 1)
    window_rows = jnp.concatenate([lower_rows, saved_rows], axis=0)
    window_state = jnp.concatenate([lower_state, saved_state], axis=0)
    local_slot = jnp.clip(source_slot - (position - 1) * slot_count, 0, 2 * slot_count - 1)
    restored = jnp.where(
        valid[:, None], jnp.take(window_rows, local_slot, axis=0), jnp.float32(0.0)
    )
    state = jnp.where(valid, jnp.take(window_state, local_slot, axis=0), jnp.float32(1.0))
    groups_total = source_rows.shape[2]
    steps_total = source_rows.shape[1]
    group_local = groups_total // lax.axis_size("rep")
    group_ids = [lax.axis_index("rep") * group_local + 0]

    def bucket_step(step_index, left_rows, state_rows, right_rows, carried):
        live_count = lax.dynamic_index_in_dim(live_groups[0], step_index, 0, keepdims=False)
        step_sources = lax.dynamic_index_in_dim(source_rows[0], step_index, 0, keepdims=False)
        step_targets = lax.dynamic_index_in_dim(target_rows[0], step_index, 0, keepdims=False)
        step_relations = lax.dynamic_index_in_dim(relation_ids[0], step_index, 0, keepdims=False)
        step_negatives = lax.dynamic_index_in_dim(negative_rows[0], step_index, 0, keepdims=False)
        group_id = group_ids[0]
        sources = lax.dynamic_index_in_dim(step_sources, group_id, 0, keepdims=False)
        targets = lax.dynamic_index_in_dim(step_targets, group_id, 0, keepdims=False)
        rel_index = lax.dynamic_index_in_dim(step_relations, group_id, 0, keepdims=False)
        negatives = lax.dynamic_index_in_dim(step_negatives, group_id, 0, keepdims=False)

        def compute_grads(operands):
            return group_grads(
                left_rows, right_rows, relations, operands[0], operands[1], operands[2], operands[3]
            )

        def empty_grads(operands):
            return (
                jnp.zeros(left_rows.shape, jnp.float32),
                jnp.zeros(left_rows.shape, jnp.float32),
            )

        grad_a, grad_b = lax.cond(
            group_id < live_count,
            compute_grads,
            empty_grads,
            (sources, targets, rel_index, negatives),
        )
        left_grad = grad_a
        right_grad = grad_b
        left_grad = left_grad + partner(left_grad, "rep", 0)
        right_grad = right_grad + partner(right_grad, "rep", 0)
        carried = carried + right_grad
        state_rows = state_rows + jnp.mean(left_grad * left_grad, axis=1)
        left_rows = left_rows - LR_RATE * left_grad / (jnp.sqrt(state_rows)[:, None] + EPSILON)
        return (left_rows, state_rows, carried)

    def cycle_body(step_index, carry_all):
        left_rows, state_rows, right_rows, carried = carry_all
        left_rows, state_rows, carried = bucket_step(
            step_index, left_rows, state_rows, right_rows, carried
        )
        moved = from_behind(jnp.stack([right_rows, carried]), "blk", 1)
        return (left_rows, state_rows, moved[0], moved[1])

    carried0 = jnp.zeros(restored.shape, jnp.float32)
    left_rows, state_rows, right_rows, carried = lax.fori_loop(
        0, steps_total - 1, cycle_body, (restored, state, restored, carried0)
    )
    left_rows, state_rows, carried = bucket_step(
        steps_total - 1, left_rows, state_rows, right_rows, carried
    )
    carried = from_behind(carried, "blk", 1 - steps_total)
    own_count = slot_count // lax.axis_size("rep")
    own_start = lax.axis_index("rep") * own_count
    left_own = lax.dynamic_slice_in_dim(left_rows, own_start, own_count, 0)
    state_own = lax.dynamic_slice_in_dim(state_rows, own_start, own_count, 0)
    carried_own = lax.dynamic_slice_in_dim(carried, own_start, own_count, 0)
    state_own = state_own + jnp.mean(carried_own * carried_own, axis=1)
    final_rows = left_own - LR_RATE * carried_own / (jnp.sqrt(state_own)[:, None] + EPSILON)
    return (final_rows, state_own)


def solution(mesh):
    return jax.shard_map(
        local,
        mesh=mesh,
        in_specs=(
            P("blk", None),
            P("blk"),
            P(),
            P(),
            P(),
            P("blk", None, None, None),
            P("blk", None, None, None),
            P("blk", None, None, None),
            P("blk", None, None, None),
            P("blk", None),
        ),
        out_specs=(P(("blk", "rep"), None), P(("blk", "rep"))),
        check_vma=False,
    )
```

profile of v0, /device:TPU:27, one launch (start us, length us, event | category | flops | bytes accessed | tf_op | source)
XLA Modules:
  0.0 872.0 jit_solution(3071964843289426359)
XLA Ops:
  0.6 3.7 collective-permute-start.4
  18.1 4.4 compare_select_fusion.16
  23.3 35.6 %select_select_fusion.1 = s32[1024]{0:T(1024)S(1)} fusion(pred[1024]{0:T(1024)(128)(4,1)S(1)} %get-tuple-element.781, pred[1024]{0:T(1024)(128)(4,1)S(1)} %get-tuple-element.779, pred[1024]{0:T(1024)(128)(4,1)S(1)} %get-tuple-element.780, pred[1024]{0:T(1024)(128)(4,1)S(1)} %get-tuple-element.778, pred[1024]{0:T(1024)(128)(4,1)S(1)} %get-tuple-element.777, ...), kind=kLoop, calls=%fused_computation.189 | loop fusion | flops 58368 | bytes 66788 | tf_op jit(solution)/shard_map/jit(_take)/gather | solution.py:77
  62.8 8.6 copy.104
  71.3 6.2 gather_fusion.9
  78.1 2.8 copy.99
  81.0 4.0 pad_maximum_fusion.5
  84.9 6.2 gather_fusion.8
  97.5 590.8 %while.22 = (s32[]{:T(128)}, f32[1024,400]{0,1:T(8,128)S(1)}, f32[1024]{0:T(1024)S(1)}, f32[1024,400]{0,1:T(8,128)}, f32[1024,400]{0,1:T(8,128)}, /*index=5*/s32...) while((s32[]{:T(128)}, f32[1024,400]{0,1:T(8,128)S(1)}, ...), condition=%wide.region_9.13_spmd, body=%wide.region_1.12_spmd.sunk | while | flops 1247727360 | bytes 176872736 | solution.py:157
  99.0 70.3 %conditional.4 = (f32[1024,400]{0,1:T(8,128)}, f32[1024,400]{0,1:T(8,128)}) conditional(s32[]{:T(128)} %convert_element_type.68, () %tuple.240, (s32[]{:T(128)}, s32[1,4,2,1000]{3,2,1,0:T(2,128)}, s32[]{:T(128)}, f32[1024,400]{0,1:T(8,128)S(1)}, s32[1,4,2,1000]{3,2,1,0:T(2,128)}, /*index=5*/f32[4131,400]{1,0:T(8,128)}, s32[1,4,2,1000]{3,2,1,0:T(2,128)}, ...), branch_computations={%region_2.2_spmd, %region_3.10_spmd} | conditional | flops 1243219712 | bytes 101481312 | solution.py:133
  99.9 8.7 gather_fusion.1
  117.0 4.9 gather_fusion.2
  121.9 2.8 copy.83
  126.5 4.9 gather_fusion
  143.2 7.8 scatter_custom_fusion.1
  150.9 4.4 scatter_fusion
  157.0 2.8 copy.84
  159.9 7.8 scatter_custom_fusion
  171.5 36.4 %collective-permute-done.1 = f32[1024,400]{0,1:T(8,128)S(1)} collective-permute-done((f32[1024,400]{0,1:T(8,128)}, f32[1024,400]{0,1:T(8,128)S(1)}, u32[]{:S(2)}, u32[]{:S(2)}) %collective-permute-start.1) | collective-permute-done | bytes 1638432 | tf_op jit(solution)/shard_map/while/body/eval_jaxpr/ppermute | solution.py:19
  215.1 71.8 %collective-permute-done = f32[1024,400]{0,1:T(8,128)S(1)} collective-permute-done((f32[1024,400]{0,1:T(8,128)}, f32[1024,400]{0,1:T(8,128)S(1)}, u32[]{:S(2)}, u32[]{:S(2)}) %collective-permute-start) | collective-permute-done | bytes 1638432 | tf_op jit(solution)/shard_map/while/body/eval_jaxpr/ppermute | solution.py:19
  290.8 4.0 slice_bitcast_fusion.3
  296.2 70.3 %conditional.4 = (f32[1024,400]{0,1:T(8,128)}, f32[1024,400]{0,1:T(8,128)}) conditional(s32[]{:T(128)} %convert_element_type.68, () %tuple.240, (s32[]{:T(128)}, s32[1,4,2,1000]{3,2,1,0:T(2,128)}, s32[]{:T(128)}, f32[1024,400]{0,1:T(8,128)S(1)}, s32[1,4,2,1000]{3,2,1,0:T(2,128)}, /*index=5*/f32[4131,400]{1,0:T(8,128)}, s32[1,4,2,1000]{3,2,1,0:T(2,128)}, ...), branch_computations={%region_2.2_spmd, %region_3.10_spmd} | conditional | flops 1243219712 | bytes 101481312 | solution.py:133
  297.0 8.7 gather_fusion.1
  314.1 4.9 gather_fusion.2
  319.0 2.8 copy.83
  323.6 4.9 gather_fusion
  340.3 7.8 scatter_custom_fusion.1
  348.1 4.4 scatter_fusion
  354.2 2.8 copy.84
  357.0 7.8 scatter_custom_fusion
  366.5 38.7 %collective-permute-done.1 = f32[1024,400]{0,1:T(8,128)S(1)} collective-permute-done((f32[1024,400]{0,1:T(8,128)}, f32[1024,400]{0,1:T(8,128)S(1)}, u32[]{:S(2)}, u32[]{:S(2)}) %collective-permute-start.1) | collective-permute-done | bytes 1638432 | tf_op jit(solution)/shard_map/while/body/eval_jaxpr/ppermute | solution.py:19
  410.2 73.5 %collective-permute-done = f32[1024,400]{0,1:T(8,128)S(1)} collective-permute-done((f32[1024,400]{0,1:T(8,128)}, f32[1024,400]{0,1:T(8,128)S(1)}, u32[]{:S(2)}, u32[]{:S(2)}) %collective-permute-start) | collective-permute-done | bytes 1638432 | tf_op jit(solution)/shard_map/while/body/eval_jaxpr/ppermute | solution.py:19
  487.5 4.0 slice_bitcast_fusion.3
  492.9 70.3 %conditional.4 = (f32[1024,400]{0,1:T(8,128)}, f32[1024,400]{0,1:T(8,128)}) conditional(s32[]{:T(128)} %convert_element_type.68, () %tuple.240, (s32[]{:T(128)}, s32[1,4,2,1000]{3,2,1,0:T(2,128)}, s32[]{:T(128)}, f32[1024,400]{0,1:T(8,128)S(1)}, s32[1,4,2,1000]{3,2,1,0:T(2,128)}, /*index=5*/f32[4131,400]{1,0:T(8,128)}, s32[1,4,2,1000]{3,2,1,0:T(2,128)}, ...), branch_computations={%region_2.2_spmd, %region_3.10_spmd} | conditional | flops 1243219712 | bytes 101481312 | solution.py:133
  493.7 8.7 gather_fusion.1
  510.9 4.9 gather_fusion.2
  520.4 4.9 gather_fusion
  537.0 7.8 scatter_custom_fusion.1
  544.8 4.4 scatter_fusion
  550.9 2.8 copy.84
  553.7 7.8 scatter_custom_fusion
  563.2 37.7 %collective-permute-done.1 = f32[1024,400]{0,1:T(8,128)S(1)} collective-permute-done((f32[1024,400]{0,1:T(8,128)}, f32[1024,400]{0,1:T(8,128)S(1)}, u32[]{:S(2)}, u32[]{:S(2)}) %collective-permute-start.1) | collective-permute-done | bytes 1638432 | tf_op jit(solution)/shard_map/while/body/eval_jaxpr/ppermute | solution.py:19
  605.7 74.3 %collective-permute-done = f32[1024,400]{0,1:T(8,128)S(1)} collective-permute-done((f32[1024,400]{0,1:T(8,128)}, f32[1024,400]{0,1:T(8,128)S(1)}, u32[]{:S(2)}, u32[]{:S(2)}) %collective-permute-start) | collective-permute-done | bytes 1638432 | tf_op jit(solution)/shard_map/while/body/eval_jaxpr/ppermute | solution.py:19
  683.8 4.0 slice_bitcast_fusion.3
  688.3 101.6 %conditional.2 = (f32[1024,400]{0,1:T(8,128)}, f32[1024,400]{0,1:T(8,128)}) conditional(s32[]{:T(128)} %convert_element_type.51, () %tuple.67, (s32[1,4,2,1000]{3,2,1,0:T(2,128)}, s32[]{:T(128)}, f32[1024,400]{0,1:T(8,128)S(1)}, s32[1,4,2,1000]{3,2,1,0:T(2,128)}, f32[4131,400]{0,1:T(8,128)}, /*index=5*/s32[1,4,2,1000]{3,2,1,0:T(2,128)}, ...), branch_computations={%region_10.14_spmd, %region_11.19_spmd} | conditional | flops 1243219712 | bytes 109841480 | solution.py:133
  691.4 2.9 copy.107
  694.3 4.2 gather_fusion.7
  698.5 6.9 gather_fusion.6
  710.0 6.9 gather_fusion.4
  719.7 2.9 broadcast_select_fusion.3
  722.6 8.5 copy.106
  731.2 8.7 gather_fusion.5
  753.8 2.8 copy.97
  756.6 8.7 scatter_custom_fusion.4
  765.3 7.3 scatter_fusion.1
  772.6 2.8 copy.121
  775.4 2.8 copy.96
  778.2 8.7 scatter_custom_fusion.3
  786.8 2.8 copy.119
  790.0 3.0 collective-permute-start.5
  792.9 35.6 %collective-permute-done.6 = f32[1024,400]{0,1:T(8,128)S(1)} collective-permute-done((f32[1024,400]{0,1:T(8,128)}, f32[1024,400]{0,1:T(8,128)S(1)}, u32[]{:S(2)}, u32[]{:S(2)}) %collective-permute-start.6) | collective-permute-done | bytes 1638432 | tf_op jit(solution)/shard_map/ppermute | solution.py:19
  828.5 3.1 add_add_fusion
  831.6 32.1 %collective-permute-done.5 = f32[1024,400]{0,1:T(8,128)} collective-permute-done((f32[1024,400]{0,1:T(8,128)}, f32[1024,400]{0,1:T(8,128)}, u32[]{:S(2)}, u32[]{:S(2)}) %collective-permute-start.5) | collective-permute-done | bytes 1638432 | tf_op jit(solution)/shard_map/ppermute | solution.py:19
  866.1 3.7 collective-permute-done.7
  (245 shorter events, 165.7 us)
Async XLA Ops:
  0.6 70.7 %collective-permute-start.4 = (f32[1024]{0:T(1024)}, f32[1024]{0:T(1024)S(1)}, u32[]{:S(2)}, u32[]{:S(2)}) collective-permute-start(f32[1024]{0:T(1024)} %param.23), channel_id=1, source_target_pairs={{0,2},{2,4},{4,6},{6,8},{8,10},{10,12},{12,14},{14,16},{16,18},{18... | collective-permute-start | bytes 12296 | tf_op jit(solution)/shard_map/ppermute | solution.py:13
  4.4 73.8 %collective-permute-start.3 = (f32[1024,400]{0,1:T(8,128)}, f32[1024,400]{0,1:T(8,128)}, u32[]{:S(2)}, u32[]{:S(2)}) collective-permute-start(f32[1024,400]{0,1:T(8,128)} %param.22), channel_id=1, source_target_pairs={{0,2},{2,4},{4,6},{6,8},{8,10},{10,12},{12,14},{14,16},{16,18},{18... | collective-permute-start | bytes 4915208 | tf_op jit(solution)/shard_map/ppermute | solution.py:13
  59.5 1.9 copy-start.11
  62.7 8.6 copy-start.10
  97.6 1.4 copy-start.2
  99.1 9.5 %copy-start.4 = (f32[1024,400]{0,1:T(8,128)}, f32[1024,400]{0,1:T(8,128)S(1)}, u32[]{:S(2)}) copy-start(f32[1024,400]{0,1:T(8,128)S(1)} %get-tuple-element.694) | copy-start | bytes 4915204 | tf_op jit(solution)/shard_map/while/body/eval_jaxpr/cond
  133.5 1.4 copy-start.1
  134.9 1.4 copy-start
  169.3 38.6 %collective-permute-start.1 = (f32[1024,400]{0,1:T(8,128)}, f32[1024,400]{0,1:T(8,128)S(1)}, u32[]{:S(2)}, u32[]{:S(2)}) collective-permute-start(f32[1024,400]{0,1:T(8,128)} %get-tuple-element.1000), channel_id=1, source_target_pairs={{0,1},{1,0},{2,3},{3,2},{4,5},{5,4},{6,7},{7,6},{8,9},{9,8},{10,11... | collective-permute-start | bytes 4915208 | tf_op jit(solution)/shard_map/while/body/eval_jaxpr/ppermute | solution.py:19
  207.9 2.5 copy-start.5
  212.6 78.2 %collective-permute-start.2 = (f32[2,1024,400]{1,2,0:T(8,128)}, f32[2,1024,400]{1,2,0:T(8,128)}, u32[]{:S(2)}, u32[]{:S(2)}) collective-permute-start(f32[2,1024,400]{1,2,0:T(8,128)} %pad_maximum_fusion.8), channel_id=1, source_target_pairs={{254,0},{0,2},{2,4},{4,6},{6,8},{8,10},{10,12},{12,14},{14,16},{16... | collective-permute-start | bytes 9830408 | tf_op jit(solution)/shard_map/while/body/eval_jaxpr/ppermute | solution.py:25
  215.1 71.8 %collective-permute-start = (f32[1024,400]{0,1:T(8,128)}, f32[1024,400]{0,1:T(8,128)S(1)}, u32[]{:S(2)}, u32[]{:S(2)}) collective-permute-start(f32[1024,400]{0,1:T(8,128)} %get-tuple-element.997), channel_id=1, source_target_pairs={{0,1},{1,0},{2,3},{3,2},{4,5},{5,4},{6,7},{7,6},{8,9},{9,8},{10,11... | collective-permute-start | bytes 4915208 | tf_op jit(solution)/shard_map/while/body/eval_jaxpr/ppermute | solution.py:19
  215.1 73.4 %copy-start.3 = (f32[1024,400]{0,1:T(8,128)S(1)}, f32[1024,400]{0,1:T(8,128)}, u32[]{:S(2)}) copy-start(f32[1024,400]{0,1:T(8,128)} %copy-done.2) | copy-start | bytes 4915204 | tf_op jit(solution)/shard_map/while
  294.8 1.3 copy-start.2
  296.2 9.5 %copy-start.4 = (f32[1024,400]{0,1:T(8,128)}, f32[1024,400]{0,1:T(8,128)S(1)}, u32[]{:S(2)}) copy-start(f32[1024,400]{0,1:T(8,128)S(1)} %get-tuple-element.694) | copy-start | bytes 4915204 | tf_op jit(solution)/shard_map/while/body/eval_jaxpr/cond
  330.6 1.4 copy-start.1
  332.0 1.4 copy-start
  366.5 38.7 %collective-permute-start.1 = (f32[1024,400]{0,1:T(8,128)}, f32[1024,400]{0,1:T(8,128)S(1)}, u32[]{:S(2)}, u32[]{:S(2)}) collective-permute-start(f32[1024,400]{0,1:T(8,128)} %get-tuple-element.1000), channel_id=1, source_target_pairs={{0,1},{1,0},{2,3},{3,2},{4,5},{5,4},{6,7},{7,6},{8,9},{9,8},{10,11... | collective-permute-start | bytes 4915208 | tf_op jit(solution)/shard_map/while/body/eval_jaxpr/ppermute | solution.py:19
  405.2 2.5 copy-start.5
  409.9 77.7 %collective-permute-start.2 = (f32[2,1024,400]{1,2,0:T(8,128)}, f32[2,1024,400]{1,2,0:T(8,128)}, u32[]{:S(2)}, u32[]{:S(2)}) collective-permute-start(f32[2,1024,400]{1,2,0:T(8,128)} %pad_maximum_fusion.8), channel_id=1, source_target_pairs={{254,0},{0,2},{2,4},{4,6},{6,8},{8,10},{10,12},{12,14},{14,16},{16... | collective-permute-start | bytes 9830408 | tf_op jit(solution)/shard_map/while/body/eval_jaxpr/ppermute | solution.py:25
  409.9 73.8 %collective-permute-start = (f32[1024,400]{0,1:T(8,128)}, f32[1024,400]{0,1:T(8,128)S(1)}, u32[]{:S(2)}, u32[]{:S(2)}) collective-permute-start(f32[1024,400]{0,1:T(8,128)} %get-tuple-element.997), channel_id=1, source_target_pairs={{0,1},{1,0},{2,3},{3,2},{4,5},{5,4},{6,7},{7,6},{8,9},{9,8},{10,11... | collective-permute-start | bytes 4915208 | tf_op jit(solution)/shard_map/while/body/eval_jaxpr/ppermute | solution.py:19
  410.2 75.2 %copy-start.3 = (f32[1024,400]{0,1:T(8,128)S(1)}, f32[1024,400]{0,1:T(8,128)}, u32[]{:S(2)}) copy-start(f32[1024,400]{0,1:T(8,128)} %copy-done.2) | copy-start | bytes 4915204 | tf_op jit(solution)/shard_map/while
  491.6 1.3 copy-start.2
  492.9 9.5 %copy-start.4 = (f32[1024,400]{0,1:T(8,128)}, f32[1024,400]{0,1:T(8,128)S(1)}, u32[]{:S(2)}) copy-start(f32[1024,400]{0,1:T(8,128)S(1)} %get-tuple-element.694) | copy-start | bytes 4915204 | tf_op jit(solution)/shard_map/while/body/eval_jaxpr/cond
  527.3 1.4 copy-start.1
  528.8 1.4 copy-start
  563.2 37.8 %collective-permute-start.1 = (f32[1024,400]{0,1:T(8,128)}, f32[1024,400]{0,1:T(8,128)S(1)}, u32[]{:S(2)}, u32[]{:S(2)}) collective-permute-start(f32[1024,400]{0,1:T(8,128)} %get-tuple-element.1000), channel_id=1, source_target_pairs={{0,1},{1,0},{2,3},{3,2},{4,5},{5,4},{6,7},{7,6},{8,9},{9,8},{10,11... | collective-permute-start | bytes 4915208 | tf_op jit(solution)/shard_map/while/body/eval_jaxpr/ppermute | solution.py:19
  601.0 2.5 copy-start.5
  605.6 78.2 %collective-permute-start.2 = (f32[2,1024,400]{1,2,0:T(8,128)}, f32[2,1024,400]{1,2,0:T(8,128)}, u32[]{:S(2)}, u32[]{:S(2)}) collective-permute-start(f32[2,1024,400]{1,2,0:T(8,128)} %pad_maximum_fusion.8), channel_id=1, source_target_pairs={{254,0},{0,2},{2,4},{4,6},{6,8},{8,10},{10,12},{12,14},{14,16},{16... | collective-permute-start | bytes 9830408 | tf_op jit(solution)/shard_map/while/body/eval_jaxpr/ppermute | solution.py:25
  605.7 74.3 %collective-permute-start = (f32[1024,400]{0,1:T(8,128)}, f32[1024,400]{0,1:T(8,128)S(1)}, u32[]{:S(2)}, u32[]{:S(2)}) collective-permute-start(f32[1024,400]{0,1:T(8,128)} %get-tuple-element.997), channel_id=1, source_target_pairs={{0,1},{1,0},{2,3},{3,2},{4,5},{5,4},{6,7},{7,6},{8,9},{9,8},{10,11... | collective-permute-start | bytes 4915208 | tf_op jit(solution)/shard_map/while/body/eval_jaxpr/ppermute | solution.py:19
  605.7 76.0 %copy-start.3 = (f32[1024,400]{0,1:T(8,128)S(1)}, f32[1024,400]{0,1:T(8,128)}, u32[]{:S(2)}) copy-start(f32[1024,400]{0,1:T(8,128)} %copy-done.2) | copy-start | bytes 4915204 | tf_op jit(solution)/shard_map/while
  688.3 140.2 %copy-start.6 = (f32[1024,400]{0,1:T(8,128)S(1)}, f32[1024,400]{0,1:T(8,128)}, u32[]{:S(2)}) copy-start(f32[1024,400]{0,1:T(8,128)} %get-tuple-element.617) | copy-start | bytes 4915204
  742.6 1.9 copy-start.8
  744.5 1.4 copy-start.7
  746.0 1.0 copy-start.9
  789.9 38.7 %collective-permute-start.6 = (f32[1024,400]{0,1:T(8,128)}, f32[1024,400]{0,1:T(8,128)S(1)}, u32[]{:S(2)}, u32[]{:S(2)}) collective-permute-start(f32[1024,400]{0,1:T(8,128)} %get-tuple-element.724), channel_id=1, source_target_pairs={{0,1},{1,0},{2,3},{3,2},{4,5},{5,4},{6,7},{7,6},{8,9},{9,8},{10,11... | collective-permute-start | bytes 4915208 | tf_op jit(solution)/shard_map/ppermute | solution.py:19
  790.0 73.8 %collective-permute-start.5 = (f32[1024,400]{0,1:T(8,128)}, f32[1024,400]{0,1:T(8,128)}, u32[]{:S(2)}, u32[]{:S(2)}) collective-permute-start(f32[1024,400]{0,1:T(8,128)} %get-tuple-element.723), channel_id=1, source_target_pairs={{0,1},{1,0},{2,3},{3,2},{4,5},{5,4},{6,7},{7,6},{8,9},{9,8},{10,11... | collective-permute-start | bytes 4915208 | tf_op jit(solution)/shard_map/ppermute | solution.py:19
  831.6 38.2 %collective-permute-start.7 = (f32[1024,400]{0,1:T(8,128)}, f32[1024,400]{0,1:T(8,128)S(1)}, u32[]{:S(2)}, u32[]{:S(2)}) collective-permute-start(f32[1024,400]{0,1:T(8,128)} %add_add_fusion), channel_id=1, source_target_pairs={{6,0},{8,2},{10,4},{12,6},{14,8},{16,10},{18,12},{20,14},{22,16},{... | collective-permute-start | bytes 4915208 | tf_op jit(solution)/shard_map/ppermute | solution.py:25
where the time goes:
time: 884 us; the launch traced here: 872 us
  waiting for transfers between devices  404 us (46%)
  local copies, waits for them, and re-layouts  244 us (28%)
  other arithmetic  192 us (22%)
  starting transfers between devices  13.7 us (2%)
  matrix products  11.6 us (1%)
    ppermute x8, waiting for transfers between devices, partner(): return lax.ppermute(value, axis, pairs)  400 us
    scatter-add x8, other arithmetic, group_grads(): right_grad = jnp.zeros(right_table.shape, jnp.float32).at[targets].add(gr...  52.3 us
    gather x8, local copies, waits for them, and re-layouts, group_grads(): rel_emb = jnp.take(relations, rel_index, axis=0)  43.7 us
    gather x3, other arithmetic, restore_slots(): jnp.take(old_starts, partition)  40.7 us
    gather x8, local copies, waits for them, and re-layouts, group_grads(): dst_emb = jnp.take(right_table, targets, axis=0)  32.7 us
    scatter-add x4, other arithmetic, group_grads(): jnp.zeros(left_table.shape, jnp.float32).at[sources].add(grad_src)  31.9 us
    gather x8, local copies, waits for them, and re-layouts, group_grads(): src_emb = jnp.take(left_table, sources, axis=0)  30.5 us
    another operation x9, local copies, waits for them, and re-layouts  24.3 us
  transfers between devices with their start and end apart: 14, of which 9 were waited for; matrix products, arithmetic and copies ran while one was open for 10% of the time, Pallas kernels for 0%

commit v1 on v0

v1 whole, which is shorter than its diff:
```python
import functools

import jax
import jax.numpy as jnp
from jax import lax
from jax.experimental import pallas as pl
from jax.experimental.pallas import tpu as pltpu
from jax.sharding import PartitionSpec as P

LR = 0.2
EPS = 1e-10
F32 = jnp.float32
BF = jnp.bfloat16
D = 400
H = 200
CAP = 1024
HALF = 512
E = 1024
N = 512
CH = 512
LOW = 192
OLD_CAP = 2048
ENTITIES = 122880
STEPS = 4
MESH = pl.DeviceIdType.MESH
ROWS_W = 512
VMEM_LIMIT = 62 * 1024 * 1024
NT = (((1,), (1,)), ((), ()))
NN = (((1,), (0,)), ((), ()))
BOTH = ("blk", "rep")
VMEM = pl.BlockSpec(memory_space=pltpu.VMEM)
ANY = pl.BlockSpec(memory_space=pl.ANY)
SMEM = pl.BlockSpec(memory_space=pltpu.SMEM)


def dot(a, b, dims):
    return lax.dot_general(a, b, dims, preferred_element_type=F32)


def split_to(ref, col, x):
    hi = x.astype(BF)
    ref[0:D, col] = hi
    ref[D : 2 * D, col] = (x - hi.astype(F32)).astype(BF)


def remote(src, dst, send, recv, device):
    return pltpu.make_async_remote_copy(
        src_ref=src, dst_ref=dst, send_sem=send, recv_sem=recv, device_id=device,
        device_id_type=MESH)


def train_kernel(blocks, ids, idx, own, own_state, rel, out, out_state,
                 tab, st, rel_s, rel_t, rows, left, state, lhl, rhl, ohs, oht, gshl, gdhl,
                 q_s, g_s, qb_s, dn_s, glo, gli, gro, gri, gsum, carr, lfin, sfin,
                 local_sem, tab_send, tab_recv, gl_send, gl_recv, gr_send, gr_recv,
                 home_send, home_recv, fin_send, fin_recv):
    b = lax.axis_index("blk")
    r = lax.axis_index("rep")
    c = lax.rem(b, 2)
    m2 = b - c
    sibling = (m2 + 1 - c, r)
    ahead = (lax.rem(b + 2, blocks), r)
    behind = (lax.rem(b + blocks - 2, blocks), r)
    here = c == r
    mine = pl.ds(pl.multiple_of(c * HALF, HALF), HALF)
    theirs = pl.ds(pl.multiple_of((1 - c) * HALF, HALF), HALF)

    def home(s):
        return (lax.rem(m2 + r - s + blocks, blocks), c)

    def origin(s):
        i = lax.rem(b + s, blocks)
        odd = lax.rem(i, 2)
        return (i - odd + r, odd)

    get_rel = pltpu.make_async_copy(rel, rel_s, local_sem.at[0])
    get_own = pltpu.make_async_copy(own, tab.at[0], local_sem.at[1])
    get_state = pltpu.make_async_copy(own_state, st.at[0], local_sem.at[2])
    get_own.start()
    get_state.start()
    get_rel.start()

    barrier = pltpu.get_barrier_semaphore()
    pl.semaphore_signal(barrier, inc=1, device_id=sibling, device_id_type=MESH)
    pl.semaphore_signal(barrier, inc=1, device_id=behind, device_id_type=MESH)
    for s in range(1, STEPS):
        pl.semaphore_signal(barrier, inc=1, device_id=origin(s), device_id_type=MESH)

    @pl.when(jnp.logical_not(here))
    def _():
        pl.semaphore_signal(barrier, inc=1, device_id=origin(0), device_id_type=MESH)

    pl.semaphore_wait(barrier, STEPS + 2 - here.astype(jnp.int32))

    share = remote(tab.at[0], tab.at[1], tab_send.at[0], tab_recv.at[0], sibling)
    share_state = remote(st.at[0], st.at[1], tab_send.at[1], tab_recv.at[1], sibling)
    onward = remote(tab.at[0], tab.at[2], tab_send.at[2], tab_recv.at[2], ahead)
    share_on = remote(tab.at[2], tab.at[3], tab_send.at[3], tab_recv.at[3], sibling)
    far = remote(tab.at[3 - c, :, mine], tab.at[4, :, mine], tab_send.at[4], tab_recv.at[4], ahead)
    share_far = remote(tab.at[4, :, mine], tab.at[4, :, mine], tab_send.at[5], tab_recv.at[5], sibling)
    share_far_in = remote(tab.at[4, :, theirs], tab.at[4, :, theirs], tab_send.at[5], tab_recv.at[5], sibling)

    def gl_copy(s, k):
        p = lax.rem(s, 2)
        part = theirs if k == 0 else mine
        return remote(glo.at[p, :, part], gli.at[p, :, part], gl_send.at[p, k], gl_recv.at[p, k], sibling)

    def gr_copy(s):
        p = lax.rem(s, 2)
        return remote(gro.at[p], gri.at[p], gr_send.at[p], gr_recv.at[p], sibling)

    def home_copy(s):
        p = lax.rem(s, 2)
        return remote(gsum.at[p], carr.at[s], home_send.at[p], home_recv.at[s], home(s))

    def home_local(s):
        return pltpu.make_async_copy(gsum.at[0], carr.at[0], local_sem.at[3])

    get_own.wait()
    get_state.wait()
    share.start()
    share_state.start()

    @pl.when(c == 1)
    def _():
        onward.start()

    get_rel.wait()

    def gather(s):
        def body(k, carry):
            base = pl.multiple_of(k * 128, 128)
            for i in range(128):
                rows[i : i + 1, 0:D] = rel_s[pl.ds(ids[s, base + i], 1), :]
            rel_t[:, pl.ds(base, 128)] = rows[...].T[0:D]
            return carry

        lax.fori_loop(0, E // 128, body, 0)

    gather(0)
    share.wait_recv()
    share_state.wait_recv()
    state[...] = jnp.where(here, st[0], st[1])
    for c0 in range(0, CAP, 256):
        col = pl.ds(c0, 256)
        x = jnp.where(here, tab[0, :, col], tab[1, :, col])
        left[:, col] = x
        split_to(lhl, col, x)

    def bucket(s, carry):
        p = lax.rem(s, 2)
        same = jnp.where(here, 0, 1)
        slot = jnp.where(
            s == 0, same,
            jnp.where(
                s == 1, jnp.where(r == 0, 3 - c, c),
                jnp.where(s == 2, 2 + same, jnp.where(r == 0, 4, 2 + c))))
        for c0 in range(0, CAP, 256):
            col = pl.ds(c0, 256)
            split_to(rhl, col, tab[slot, :, col])
        row_n = lax.broadcasted_iota(jnp.int32, (CAP, N), 0)
        ohn = jnp.where(row_n == idx[s, 2:3, 0:N], 1.0, 0.0).astype(BF)
        oht[:, E : E + N] = ohn
        nbt = dot(rhl[0:D, :], ohn, NN).astype(BF)
        nb = nbt.T
        for e in range(E // CH):
            col = pl.ds(e * CH, CH)
            live = idx[s, 4:5, col].astype(F32)
            row = lax.broadcasted_iota(jnp.int32, (CAP, CH), 0)
            oh_s = jnp.where(row == idx[s, 0:1, col], 1.0, 0.0).astype(BF)
            ohs[:, col] = oh_s
            sh = dot(lhl[...], oh_s, NN)
            oh_t = jnp.where(row == idx[s, 1:2, col], 1.0, 0.0).astype(BF)
            oht[:, col] = oh_t
            dh = dot(rhl[...], oh_t, NN)
            d = dh[0:D] + dh[D : 2 * D]
            s_re = sh[0:H] + sh[D : D + H]
            s_im = sh[H:D] + sh[D + H : 2 * D]
            r_re = rel_t[0:H, col]
            r_im = rel_t[H:D, col]
            q_s[0:H, :] = s_re * r_re - s_im * r_im
            q_s[H:D, :] = s_re * r_im + s_im * r_re
            q = q_s[...]
            pos = jnp.sum(q * d, axis=0, keepdims=True)
            dpos = -jax.nn.sigmoid(-pos) * live
            split_to(gdhl, col, dpos * q)
            qb = q.astype(BF)
            qb_s[:, col] = qb
            scores = dot(nb, qb, NN)
            dneg = (jax.nn.sigmoid(scores) * (live * (1.0 / N))).astype(BF)
            dn_s[:, col] = dneg
            g_s[...] = dpos * d + dot(nbt, dneg, NN)
            g_re = g_s[0:H, :]
            g_im = g_s[H:D, :]
            q_s[0:H, :] = g_re * r_re + g_im * r_im
            q_s[H:D, :] = g_im * r_re - g_re * r_im
            split_to(gshl, col, q_s[...])
        split_to(gdhl, pl.ds(E, N), dot(qb_s[...], dn_s[...], NT))

        def right_half(part):
            y = dot(gdhl[...], oht[part, :], NT)
            return y[0:D] + y[D : 2 * D]

        def left_half(part):
            y = dot(gshl[...], ohs[part, :], NT)
            glo[p, :, part] = y[0:D] + y[D : 2 * D]

        gro[p] = right_half(theirs)
        gr_copy(s).start()
        gsum[p] = right_half(mine)
        left_half(theirs)
        gl_copy(s, 0).start()
        gr_copy(s).wait()
        gsum[p] = gsum[p] + gri[p]

        @pl.when(jnp.logical_and(s == 0, here))
        def _():
            home_local(s).start()

        @pl.when(jnp.logical_or(s > 0, jnp.logical_not(here)))
        def _():
            home_copy(s).start()

        left_half(mine)

        @pl.when(s < STEPS - 1)
        def _():
            gl_copy(s, 1).start()
            gather(s + 1)

        @pl.when(s == 0)
        def _():
            @pl.when(c == 0)
            def _():
                onward.start()
                share_on.wait_recv()

            @pl.when(c == 1)
            def _():
                onward.wait_recv()
                share_on.start()

        @pl.when(s == 1)
        def _():
            @pl.when(r == 0)
            def _():
                far.start()

            @pl.when(c == 0)
            def _():
                onward.wait_recv()
                share_on.start()

            @pl.when(c == 1)
            def _():
                share_on.wait_recv()

        @pl.when(jnp.logical_and(s == 2, r == 0))
        def _():
            far.wait_recv()
            share_far.start()
            share_far_in.wait_recv()

        @pl.when(jnp.logical_and(s == 1, here))
        def _():
            home_local(s).wait()

        @pl.when(jnp.logical_and(s == 1, jnp.logical_not(here)))
        def _():
            home_copy(0).wait_send()

        @pl.when(s > 1)
        def _():
            home_copy(s - 1).wait_send()

        gl_copy(s, 0).wait_send()
        gl_in = remote(glo.at[p, :, mine], gli.at[p, :, mine], gl_send.at[p, 0], gl_recv.at[p, 0], sibling)
        gl_in.wait_recv()

        @pl.when(s < STEPS - 1)
        def _():
            gl_copy(s, 1).wait_send()
            other = remote(glo.at[p, :, theirs], gli.at[p, :, theirs], gl_send.at[p, 1], gl_recv.at[p, 1], sibling)
            other.wait_recv()
            for c0 in range(0, CAP, 256):
                col = pl.ds(c0, 256)
                g = glo[p, :, col] + gli[p, :, col]
                v = state[:, col] + jnp.sum(g * g, axis=0, keepdims=True) * (1.0 / D)
                x = left[:, col] - LR * g / (jnp.sqrt(v[0:1]) + EPS)
                state[:, col] = v
                left[:, col] = x
                split_to(lhl, col, x)

        return carry

    lax.fori_loop(0, STEPS, bucket, 0)

    p = (STEPS - 1) % 2
    g = glo[p, :, mine] + gli[p, :, mine]
    v = state[:, mine] + jnp.sum(g * g, axis=0, keepdims=True) * (1.0 / D)
    lfin[0] = left[:, mine] - LR * g / (jnp.sqrt(v[0:1]) + EPS)
    sfin[0] = v
    fin = remote(lfin.at[0], lfin.at[1], fin_send.at[0], fin_recv.at[0], home(0))
    fin_state = remote(sfin.at[0], sfin.at[1], fin_send.at[1], fin_recv.at[1], home(0))
    fin_here = pltpu.make_async_copy(lfin.at[0], lfin.at[1], local_sem.at[0])
    fin_state_here = pltpu.make_async_copy(sfin.at[0], sfin.at[1], local_sem.at[1])

    @pl.when(here)
    def _():
        fin_here.start()
        fin_state_here.start()

    @pl.when(jnp.logical_not(here))
    def _():
        fin.start()
        fin_state.start()
        home_copy(0).wait_recv()

    share.wait_send()
    share_state.wait_send()
    onward.wait_send()
    share_on.wait_send()

    @pl.when(r == 0)
    def _():
        far.wait_send()
        share_far.wait_send()

    for s in range(1, STEPS):
        home_copy(s).wait_recv()
    total = (carr[0] + carr[1]) + (carr[2] + carr[3])

    @pl.when(here)
    def _():
        fin_here.wait()
        fin_state_here.wait()

    @pl.when(jnp.logical_not(here))
    def _():
        fin.wait()
        fin_state.wait()

    v = sfin[1] + jnp.sum(total * total, axis=0, keepdims=True) * (1.0 / D)
    out[...] = lfin[1] - LR * total / (jnp.sqrt(v[0:1]) + EPS)
    out_state[...] = v
    home_copy(STEPS - 1).wait_send()


def train_call(blocks, ids, idx, own, own_state, rel):
    dma = pltpu.SemaphoreType.DMA
    return pl.pallas_call(
        functools.partial(train_kernel, blocks),
        out_shape=(jax.ShapeDtypeStruct((D, HALF), F32), jax.ShapeDtypeStruct((8, HALF), F32)),
        in_specs=[SMEM, VMEM, ANY, ANY, ANY],
        out_specs=(VMEM, VMEM),
        scratch_shapes=[
            pltpu.VMEM((5, D, CAP), F32),
            pltpu.VMEM((2, 8, CAP), F32),
            pltpu.VMEM(rel.shape, F32),
            pltpu.VMEM((D, E), F32),
            pltpu.VMEM((128, ROWS_W), F32),
            pltpu.VMEM((D, CAP), F32),
            pltpu.VMEM((8, CAP), F32),
            pltpu.VMEM((2 * D, CAP), BF),
            pltpu.VMEM((2 * D, CAP), BF),
            pltpu.VMEM((CAP, E), BF),
            pltpu.VMEM((CAP, E + N), BF),
            pltpu.VMEM((2 * D, E), BF),
            pltpu.VMEM((2 * D, E + N), BF),
            pltpu.VMEM((D, CH), F32),
            pltpu.VMEM((D, CH), F32),
            pltpu.VMEM((D, E), BF),
            pltpu.VMEM((N, E), BF),
            pltpu.VMEM((2, D, CAP), F32),
            pltpu.VMEM((2, D, CAP), F32),
            pltpu.VMEM((2, D, HALF), F32),
            pltpu.VMEM((2, D, HALF), F32),
            pltpu.VMEM((2, D, HALF), F32),
            pltpu.VMEM((STEPS, D, HALF), F32),
            pltpu.VMEM((2, D, HALF), F32),
            pltpu.VMEM((2, 8, HALF), F32),
            dma((4,)),
            dma((6,)),
            dma((6,)),
            dma((2, 2)),
            dma((2, 2)),
            dma((2,)),
            dma((2,)),
            dma((2,)),
            dma((STEPS,)),
            dma((2,)),
            dma((2,)),
        ],
        compiler_params=pltpu.CompilerParams(
            vmem_limit_bytes=VMEM_LIMIT, collective_id=0, has_side_effects=True),
        cost_estimate=pl.CostEstimate(flops=4 * 10**10, bytes_accessed=10**7, transcendentals=0),
        name="train",
    )(ids, idx, own, own_state, rel)


def local(blocks, saved_rows, saved_state, old_starts, new_starts, relations,
          source_rows, target_rows, relation_ids, negative_rows, live_groups):
    b = lax.axis_index("blk")
    r = lax.axis_index("rep")
    c = b % 2

    def move(x, route):
        pairs = []
        for m in range(blocks // 2):
            for rr in range(2):
                for cc in range(2):
                    to = route(m, rr, cc)
                    if to is not None:
                        tb, tr = to
                        pairs.append(((2 * m + cc) * 2 + rr, (tb % blocks) * 2 + tr))
        return lax.ppermute(x, BOTH, pairs)

    def sibling(x):
        return move(x, lambda m, rr, cc: (2 * m + 1 - cc, rr))

    def pad(x, fill=-1):
        return jnp.pad(x, ((0, 0), (0, E - x.shape[1])), constant_values=fill)[:, None]

    def pack(g):
        def one(x):
            return pad(lax.dynamic_index_in_dim(x[0], g, 1, keepdims=False))

        rels = pad(lax.dynamic_index_in_dim(relation_ids[0], g, 1, keepdims=False), 0)
        alive = (g < live_groups[0]).astype(jnp.int32)[:, None]
        alive = pad(jnp.broadcast_to(alive, (STEPS, source_rows.shape[3])), 0)
        parts = [one(source_rows), one(target_rows), one(negative_rows), rels, alive]
        return jnp.concatenate(parts + [jnp.zeros((STEPS, 3, E), jnp.int32)], axis=1)

    theirs = sibling(pack(1 - c))
    idx = jnp.where(c == r, pack(c), theirs)

    table = saved_rows.T
    last = old_starts.shape[0] - 1

    def tail_end(q):
        p = q // 2
        even = old_starts[p] - old_starts[jnp.maximum(p - 1, 0)] - CAP
        return jnp.where(q % 2 == 1, CAP, even)

    nxt = jnp.minimum(b + 1, blocks - 1)
    cut = jnp.clip(tail_end(nxt) - LOW, 0, CAP - LOW)
    low_t = lax.dynamic_slice(table, (0, cut), (D, LOW))
    low_s = lax.dynamic_slice(saved_state, (cut,), (LOW,))
    shift = [(((q - 1) * 2 + rr), q * 2 + rr) for q in range(1, blocks) for rr in range(2)]
    low_t = lax.ppermute(low_t, BOTH, shift)
    low_s = lax.ppermute(low_s, BOTH, shift)
    first = new_starts[b]
    end = jnp.where(b + 1 < blocks, new_starts[nxt], ENTITIES)
    p = jnp.minimum(b // 2, last)
    k = jnp.where(b % 2 == 1, CAP - (first - old_starts[p]), old_starts[p] - first)
    begin = jnp.clip(LOW - k, 0, LOW)
    valid = jnp.arange(CAP, dtype=jnp.int32)[None] < end - first
    own = lax.dynamic_slice(jnp.concatenate([low_t, table], axis=1), (0, begin), (D, CAP))
    own = jnp.where(valid, own, 0.0)
    own_s = lax.dynamic_slice(jnp.concatenate([low_s, saved_state])[None], (0, begin), (1, CAP))
    own_s = jnp.where(valid, own_s, 1.0)

    rows8 = jnp.broadcast_to(own_s, (8, CAP))
    left, state = train_call(blocks, idx[:, 3], idx, own, rows8, relations)
    return left.T, state[0]


def solution(mesh):
    return jax.shard_map(
        functools.partial(local, mesh.shape["blk"]),
        mesh=mesh,
        in_specs=(
            P("blk", None),
            P("blk"),
            P(),
            P(),
            P(),
            P("blk", None, None, None),
            P("blk", None, None, None),
            P("blk", None, None, None),
            P("blk", None, None, None),
            P("blk", None),
        ),
        out_specs=(P(("blk", "rep"), None), P(("blk", "rep"))),
        check_vma=False,
    )
```

time: 884 us -> 159 us (0.18); the launches traced: 872 us -> 156 us
  waiting for transfers between devices: 404 us -> 0.01 us
  local copies, waits for them, and re-layouts: 244 us -> 20.7 us
  other arithmetic: 192 us -> 2.6 us
  Pallas kernels: 0 us -> 119 us
  matrix products: 11.6 us -> 0 us
    ppermute x14 -> x3, waiting for transfers between devices: 404 us -> 0.01 us  [the longest x1 0.01 us: move(): return lax.ppermute(x, BOTH, pairs)]
    gather x34 -> x0, local copies, waits for them, and re-layouts: 136 us -> none  [the longest x8 43.7 us: group_grads(): rel_emb = jnp.take(relations, rel_index, axis=0)]
    pallas_call x0 -> x1, Pallas kernels: none -> 119 us  [train_call(): pl.pallas_call(functools.partial(train_kernel, blocks), out_shape=(jax.Sh...]
    scatter-add x12 -> x0, other arithmetic: 84.3 us -> none  [the longest x8 52.3 us: group_grads(): right_grad = jnp.zeros(right_table.shape, jnp.float32).at[targets].add(gr...]
    gather x20 -> x0, other arithmetic: 40.8 us -> none  [the longest x3 40.7 us: restore_slots(): jnp.take(old_starts, partition)]
    cond x32 -> x0, local copies, waits for them, and re-layouts: 24.6 us -> none  [the longest x8 15.9 us: bucket_step(): lax.cond(group_id < live_count, compute_grads, empty_grads, (sources, tar...]
    another operation x9 -> x1, local copies, waits for them, and re-layouts: 24.3 us -> 0.01 us
    select_n x35 -> x3, other arithmetic: 16.7 us -> 1.93 us  [the longest x1 1.83 us: local(): own = jnp.where(valid, own, 0.0)]
  transfers between devices with their start and end apart: 14 -> 3, of which waited for: 9 -> 0; matrix products, arithmetic and copies ran while one was open for 10% -> 10% of each run, Pallas kernels for 0% -> 0%
where the time goes in v1:
time: 159 us; the launch traced here: 156 us
  Pallas kernels  119 us (75%)
  local copies, waits for them, and re-layouts  20.7 us (13%)
  starting transfers between devices  7.32 us (5%)
  between operations  6.18 us (4%)
  other arithmetic  2.6 us (2%)
    pallas_call x1, Pallas kernels, train_call(): pl.pallas_call(functools.partial(train_kernel, blocks), out_shape=(jax.Sh...  119 us
    unnamed x17, local copies, waits for them, and re-layouts  11.4 us
    ppermute x1, starting transfers between devices, local(): low_s = lax.ppermute(low_s, BOTH, shift)  3.72 us
    ppermute x1, starting transfers between devices, local(): low_t = lax.ppermute(low_t, BOTH, shift)  3.5 us
  transfers between devices with their start and end apart: 3, of which 0 were waited for; matrix products, arithmetic and copies ran while one was open for 10% of the time, Pallas kernels for 0%

profile of v1, /device:TPU:27, one launch (start us, length us, event | category | flops | bytes accessed | tf_op | source)
XLA Modules:
  0.0 156.2 jit_solution(13308036295442378922)
XLA Ops:
  0.6 0.0 copy-start.3
  0.7 1.4 fusion.7
  3.4 0.8 dynamic_slice.67
  4.2 3.7 %collective-permute-start.2 = (f32[192]{0:T(256)S(1)}, f32[192]{0:T(256)S(1)}, u32[]{:S(2)}, u32[]{:S(2)}) collective-permute-start(f32[192]{0:T(256)S(1)} %dynamic_slice.67), channel_id=1, source_target_pairs={{0,2},{1,3},{2,4},{3,5},{4,6},{5,7},{6,8},{7,9},{8,10},{9,11},{10,... | collective-permute-start | bytes 2312 | tf_op jit(solution)/shard_map/ppermute | solution.py:451
  7.9 0.7 fusion.5
  8.6 0.1 broadcast_in_dim.75
  8.7 0.8 constant_dynamic-slice_fusion.1
  9.6 0.9 constant_dynamic-slice_fusion.3
  10.5 0.9 constant_dynamic-slice_fusion
  11.5 0.2 concatenate.13
  11.7 0.1 collective-permute-start
  11.8 1.3 dynamic-slice_bitcast_fusion
  13.0 3.5 %collective-permute-start.1 = (f32[400,192]{1,0:T(8,128)S(1)}, f32[400,192]{1,0:T(8,128)S(1)}, u32[]{:S(2)}, u32[]{:S(2)}) collective-permute-start(f32[400,192]{1,0:T(8,128)S(1)} %dynamic-slice_bitcast_fusion), channel_id=1, source_target_pairs={{0,2},{1,3},{2,4},{3,5},{4,6},{5,7},{6,8},{7,9},{8,10},{9,11},{10,... | collective-permute-start | bytes 921608 | tf_op jit(solution)/shard_map/ppermute | solution.py:450
  16.6 0.0 copy-done.3
  16.6 0.6 fusion.6
  21.0 0.1 broadcast_in_dim.69
  21.3 0.0 copy-start.2
  21.3 0.0 copy-start
  21.3 8.7 %copy.13.rel = f32[4131,400]{1,0:T(8,128)} copy(f32[4131,400]{0,1:T(8,128)} %param.14) | data formatting | bytes 13219200 | tf_op args[4]
  30.0 0.2 concatenate.12
  30.2 0.0 collective-permute-done.2
  30.2 0.0 copy-done.2
  30.2 0.1 fusion.3
  30.3 0.0 collective-permute-done
  30.3 0.0 copy-start.1
  30.3 0.6 copy.32
  30.9 0.0 collective-permute-done.1
  30.9 0.0 copy-done
  30.9 1.8 %fusion.1.own = f32[400,1024]{1,0:T(8,128)} fusion(s32[]{:T(128)S(6)} %min.16, f32[400,192]{1,0:T(8,128)S(1)} %collective-permute-done.1, f32[400,1024]{1,0:T(8,128)S(1)} %bitcast.36, pred[1024]{0:T(1024)(128)(4,1)S(1)} %iota_compare_fusion), kind=kLoop, calls=%fused_computation.3 | loop fusion | flops 819200 | bytes 3585028 | tf_op jit(solution)/shard_map/jit(_where)/select_n | solution.py:459
  32.8 0.0 copy-done.1
  32.8 0.6 broadcast_in_dim.80.own_state
  33.4 119.4 %train.1 = (f32[400,512]{1,0:T(8,128)}, f32[8,512]{1,0:T(8,128)}) custom-call(s32[4,1024]{1,0:T(4,128)} %bitcast.42, s32[4,8,1024]{2,1,0:T(8,128)} %copy-done.1, f32[400,1024]{1,0:T(8,128)} %fusion.1.own, f32[8,1024]{1,0:T(8,128)} %broadcast_in_dim.80.own_state, f32[4131,400]{1,0:T(8,128)} %copy.13.rel), custom_call_target="tpu_custom_call" | custom-call | flops 40000000000 | bytes 10000000 | tf_op jit(solution)/shard_map/train/pallas_call | solution.py:351
  152.8 1.3 slice.7
  154.1 2.1 %copy.38 = f32[512,400]{0,1:T(8,128)} copy(f32[512,400]{0,1:T(8,128)} %bitcast.37) | data formatting | bytes 1638400
  (30 shorter events, 0.3 us)
Async XLA Ops:
  0.6 15.9 %copy-start.3 = (s32[128]{0:T(128)S(1)}, s32[128]{0:T(128)}, u32[]{:S(2)}) copy-start(s32[128]{0:T(128)} %param.13) | copy-start | bytes 1540
  4.2 26.0 %collective-permute-start.2 = (f32[192]{0:T(256)S(1)}, f32[192]{0:T(256)S(1)}, u32[]{:S(2)}, u32[]{:S(2)}) collective-permute-start(f32[192]{0:T(256)S(1)} %dynamic_slice.67), channel_id=1, source_target_pairs={{0,2},{1,3},{2,4},{3,5},{4,6},{5,7},{6,8},{7,9},{8,10},{9,11},{10,... | collective-permute-start | bytes 2312 | tf_op jit(solution)/shard_map/ppermute | solution.py:451
  11.7 18.6 %collective-permute-start = (s32[4,8,1024]{2,1,0:T(8,128)S(1)}, s32[4,8,1024]{2,1,0:T(8,128)S(1)}, u32[]{:S(2)}, u32[]{:S(2)}) collective-permute-start(s32[4,8,1024]{2,1,0:T(8,128)S(1)} %concatenate.13), channel_id=1, source_target_pairs={{0,2},{2,0},{1,3},{3,1},{4,6},{6,4},{5,7},{7,5},{8,10},{10,8},{9,1... | collective-permute-start | bytes 393224 | tf_op jit(solution)/shard_map/ppermute | solution.py:416
  13.0 17.9 %collective-permute-start.1 = (f32[400,192]{1,0:T(8,128)S(1)}, f32[400,192]{1,0:T(8,128)S(1)}, u32[]{:S(2)}, u32[]{:S(2)}) collective-permute-start(f32[400,192]{1,0:T(8,128)S(1)} %dynamic-slice_bitcast_fusion), channel_id=1, source_target_pairs={{0,2},{1,3},{2,4},{3,5},{4,6},{5,7},{6,8},{7,9},{8,10},{9,11},{10,... | collective-permute-start | bytes 921608 | tf_op jit(solution)/shard_map/ppermute | solution.py:450
  21.3 8.9 %copy-start.2 = (f32[1024]{0:T(1024)S(1)}, f32[1024]{0:T(1024)}, u32[]{:S(2)}) copy-start(f32[1024]{0:T(1024)} %param.11) | copy-start | bytes 12292
  21.3 9.6 %copy-start = (f32[1024,400]{0,1:T(8,128)S(1)}, f32[1024,400]{0,1:T(8,128)}, u32[]{:S(2)}) copy-start(f32[1024,400]{0,1:T(8,128)} %param.10) | copy-start | bytes 4915204
  30.3 2.5 %copy-start.1 = (s32[4,8,1024]{2,1,0:T(8,128)}, s32[4,8,1024]{2,1,0:T(8,128)S(1)}, u32[]{:S(2)}) copy-start(s32[4,8,1024]{2,1,0:T(8,128)S(1)} %broadcast_select_fusion.idx) | copy-start | bytes 393220

commit v2 on v1

--- a/solution.py
+++ b/solution.py
@@ -49,9 +49,9 @@
         device_id_type=MESH)
 
 
-def train_kernel(blocks, ids, idx, own, own_state, rel, out, out_state,
+def train_kernel(blocks, ids, idx, own, own_state, rel, rel_end, out, out_state,
                  tab, st, rel_s, rel_t, rows, left, state, lhl, rhl, ohs, oht, gshl, gdhl,
-                 q_s, g_s, qb_s, dn_s, glo, gli, gro, gri, gsum, carr, lfin, sfin,
+                 q_s, g_s, d_s, dp_s, qb_s, dn_s, glo, gli, gro, gri, gsum, carr, lfin, sfin,
                  local_sem, tab_send, tab_recv, gl_send, gl_recv, gr_send, gr_recv,
                  home_send, home_recv, fin_send, fin_recv):
     b = lax.axis_index("blk")
@@ -61,6 +61,8 @@
     sibling = (m2 + 1 - c, r)
     ahead = (lax.rem(b + 2, blocks), r)
     behind = (lax.rem(b + blocks - 2, blocks), r)
+    ahead_far = (lax.rem(b + 4, blocks), r)
+    behind_far = (lax.rem(b + blocks - 4, blocks), r)
     here = c == r
     mine = pl.ds(pl.multiple_of(c * HALF, HALF), HALF)
     theirs = pl.ds(pl.multiple_of((1 - c) * HALF, HALF), HALF)
@@ -73,12 +75,21 @@
         odd = lax.rem(i, 2)
         return (i - odd + r, odd)
 
-    get_rel = pltpu.make_async_copy(rel, rel_s, local_sem.at[0])
+    full = rel.shape[1] // CAP
+
+    def get_rel(k):
+        if k == full:
+            return pltpu.make_async_copy(rel_end, gro.at[0, :, 0:128], local_sem.at[0])
+        return pltpu.make_async_copy(
+            rel.at[:, k * CAP : (k + 1) * CAP], glo.at[k % 2], local_sem.at[4 + k % 2])
+
     get_own = pltpu.make_async_copy(own, tab.at[0], local_sem.at[1])
     get_state = pltpu.make_async_copy(own_state, st.at[0], local_sem.at[2])
     get_own.start()
     get_state.start()
-    get_rel.start()
+    for k in range(min(2, full)):
+        get_rel(k).start()
+    get_rel(full).start()
 
     barrier = pltpu.get_barrier_semaphore()
     pl.semaphore_signal(barrier, inc=1, device_id=sibling, device_id_type=MESH)
@@ -90,13 +101,17 @@
     def _():
         pl.semaphore_signal(barrier, inc=1, device_id=origin(0), device_id_type=MESH)
 
-    pl.semaphore_wait(barrier, STEPS + 2 - here.astype(jnp.int32))
+    @pl.when(r == 0)
+    def _():
+        pl.semaphore_signal(barrier, inc=1, device_id=behind_far, device_id_type=MESH)
+
+    pl.semaphore_wait(barrier, STEPS + 3 - r - here.astype(jnp.int32))
 
     share = remote(tab.at[0], tab.at[1], tab_send.at[0], tab_recv.at[0], sibling)
     share_state = remote(st.at[0], st.at[1], tab_send.at[1], tab_recv.at[1], sibling)
     onward = remote(tab.at[0], tab.at[2], tab_send.at[2], tab_recv.at[2], ahead)
     share_on = remote(tab.at[2], tab.at[3], tab_send.at[3], tab_recv.at[3], sibling)
-    far = remote(tab.at[3 - c, :, mine], tab.at[4, :, mine], tab_send.at[4], tab_recv.at[4], ahead)
+    far = remote(tab.at[1 - c, :, mine], tab.at[4, :, mine], tab_send.at[4], tab_recv.at[4], ahead_far)
     share_far = remote(tab.at[4, :, mine], tab.at[4, :, mine], tab_send.at[5], tab_recv.at[5], sibling)
     share_far_in = remote(tab.at[4, :, theirs], tab.at[4, :, theirs], tab_send.at[5], tab_recv.at[5], sibling)
 
@@ -125,7 +140,19 @@
     def _():
         onward.start()
 
-    get_rel.wait()
+    for k in range(full):
+        get_rel(k).wait()
+
+        def turn(i, carry):
+            at = pl.multiple_of(i * 128, 128)
+            rel_s[pl.ds(pl.multiple_of(k * CAP + at, 128), 128), :] = glo[k % 2, :, pl.ds(at, 128)].T
+            return carry
+
+        lax.fori_loop(0, CAP // 128, turn, 0)
+        if k + 2 < full:
+            get_rel(k + 2).start()
+    get_rel(full).wait()
+    rel_s[full * CAP :, :] = gro[0, :, 0:128].T[0 : rel.shape[1] - full * CAP]
 
     def gather(s):
         def body(k, carry):
@@ -140,6 +167,11 @@
     gather(0)
     share.wait_recv()
     share_state.wait_recv()
+
+    @pl.when(r == 0)
+    def _():
+        far.start()
+
     state[...] = jnp.where(here, st[0], st[1])
     for c0 in range(0, CAP, 256):
         col = pl.ds(c0, 256)
@@ -183,23 +215,33 @@
             q = q_s[...]
             pos = jnp.sum(q * d, axis=0, keepdims=True)
             dpos = -jax.nn.sigmoid(-pos) * live
+            d_s[:, col] = d
+            dp_s[:, col] = dpos
             split_to(gdhl, col, dpos * q)
             qb = q.astype(BF)
             qb_s[:, col] = qb
             scores = dot(nb, qb, NN)
-            dneg = (jax.nn.sigmoid(scores) * (live * (1.0 / N))).astype(BF)
-            dn_s[:, col] = dneg
-            g_s[...] = dpos * d + dot(nbt, dneg, NN)
+            dn_s[:, col] = (jax.nn.sigmoid(scores) * (live * (1.0 / N))).astype(BF)
+        split_to(gdhl, pl.ds(E, N), dot(qb_s[...], dn_s[...], NT))
+
+        @pl.when(jnp.logical_and(s == 0, c == 0))
+        def _():
+            onward.start()
+
+        def right_half(part):
+            y = dot(gdhl[...], oht[part, :], NT)
+            return y[0:D] + y[D : 2 * D]
+
+        def source_grad(e):
+            col = pl.ds(e * CH, CH)
+            r_re = rel_t[0:H, col]
+            r_im = rel_t[H:D, col]
+            g_s[...] = dp_s[:, col] * d_s[:, col] + dot(nbt, dn_s[:, col], NN)
             g_re = g_s[0:H, :]
             g_im = g_s[H:D, :]
             q_s[0:H, :] = g_re * r_re + g_im * r_im
             q_s[H:D, :] = g_im * r_re - g_re * r_im
             split_to(gshl, col, q_s[...])
-        split_to(gdhl, pl.ds(E, N), dot(qb_s[...], dn_s[...], NT))
-
-        def right_half(part):
-            y = dot(gdhl[...], oht[part, :], NT)
-            return y[0:D] + y[D : 2 * D]
 
         def left_half(part):
             y = dot(gshl[...], ohs[part, :], NT)
@@ -208,19 +250,22 @@
         gro[p] = right_half(theirs)
         gr_copy(s).start()
         gsum[p] = right_half(mine)
+        source_grad(0)
+        gr_copy(s).wait()
+        gsum[p] = gsum[p] + gri[p]
+
+        @pl.when(jnp.logical_and(s == 0, here))
+        def _():
+            home_local(s).start()
+
+        @pl.when(jnp.logical_or(s > 0, jnp.logical_not(here)))
+        def _():
+            home_copy(s).start()
+
+        for e in range(1, E // CH):
+            source_grad(e)
         left_half(theirs)
         gl_copy(s, 0).start()
-        gr_copy(s).wait()
-        gsum[p] = gsum[p] + gri[p]
-
-        @pl.when(jnp.logical_and(s == 0, here))
-        def _():
-            home_local(s).start()
-
-        @pl.when(jnp.logical_or(s > 0, jnp.logical_not(here)))
-        def _():
-            home_copy(s).start()
-
         left_half(mine)
 
         @pl.when(s < STEPS - 1)
@@ -232,7 +277,6 @@
         def _():
             @pl.when(c == 0)
             def _():
-                onward.start()
                 share_on.wait_recv()
 
             @pl.when(c == 1)
@@ -242,10 +286,6 @@
 
         @pl.when(s == 1)
         def _():
-            @pl.when(r == 0)
-            def _():
-                far.start()
-
             @pl.when(c == 0)
             def _():
                 onward.wait_recv()
@@ -342,21 +382,21 @@
 
     v = sfin[1] + jnp.sum(total * total, axis=0, keepdims=True) * (1.0 / D)
     out[...] = lfin[1] - LR * total / (jnp.sqrt(v[0:1]) + EPS)
-    out_state[...] = v
+    out_state[...] = v[0:1]
     home_copy(STEPS - 1).wait_send()
 
 
-def train_call(blocks, ids, idx, own, own_state, rel):
+def train_call(blocks, ids, idx, own, own_state, rel, rel_end):
     dma = pltpu.SemaphoreType.DMA
     return pl.pallas_call(
         functools.partial(train_kernel, blocks),
-        out_shape=(jax.ShapeDtypeStruct((D, HALF), F32), jax.ShapeDtypeStruct((8, HALF), F32)),
-        in_specs=[SMEM, VMEM, ANY, ANY, ANY],
+        out_shape=(jax.ShapeDtypeStruct((D, HALF), F32), jax.ShapeDtypeStruct((1, HALF), F32)),
+        in_specs=[SMEM, VMEM, ANY, ANY, ANY, ANY],
         out_specs=(VMEM, VMEM),
         scratch_shapes=[
             pltpu.VMEM((5, D, CAP), F32),
             pltpu.VMEM((2, 8, CAP), F32),
-            pltpu.VMEM(rel.shape, F32),
+            pltpu.VMEM(rel.shape[::-1], F32),
             pltpu.VMEM((D, E), F32),
             pltpu.VMEM((128, ROWS_W), F32),
             pltpu.VMEM((D, CAP), F32),
@@ -369,6 +409,8 @@
             pltpu.VMEM((2 * D, E + N), BF),
             pltpu.VMEM((D, CH), F32),
             pltpu.VMEM((D, CH), F32),
+            pltpu.VMEM((D, E), F32),
+            pltpu.VMEM((1, E), F32),
             pltpu.VMEM((D, E), BF),
             pltpu.VMEM((N, E), BF),
             pltpu.VMEM((2, D, CAP), F32),
@@ -379,7 +421,7 @@
             pltpu.VMEM((STEPS, D, HALF), F32),
             pltpu.VMEM((2, D, HALF), F32),
             pltpu.VMEM((2, 8, HALF), F32),
-            dma((4,)),
+            dma((6,)),
             dma((6,)),
             dma((6,)),
             dma((2, 2)),
@@ -395,7 +437,7 @@
             vmem_limit_bytes=VMEM_LIMIT, collective_id=0, has_side_effects=True),
         cost_estimate=pl.CostEstimate(flops=4 * 10**10, bytes_accessed=10**7, transcendentals=0),
         name="train",
-    )(ids, idx, own, own_state, rel)
+    )(ids, idx, own, own_state, rel, rel_end)
 
 
 def local(blocks, saved_rows, saved_state, old_starts, new_starts, relations,
@@ -461,7 +503,10 @@
     own_s = jnp.where(valid, own_s, 1.0)
 
     rows8 = jnp.broadcast_to(own_s, (8, CAP))
-    left, state = train_call(blocks, idx[:, 3], idx, own, rows8, relations)
+    rel = relations.T
+    end_at = rel.shape[1] // CAP * CAP
+    rel_end = jnp.pad(rel[:, end_at:], ((0, 0), (0, end_at + 128 - rel.shape[1])))
+    left, state = train_call(blocks, idx[:, 3], idx, own, rows8, rel, rel_end)
     return left.T, state[0]
 
 

time: 159 us -> 158 us (level)
  the two profiles are of different devices: /device:TPU:27 before, /device:TPU:166 now
where the time goes in v2:
time: 158 us
  Pallas kernels  128 us (81%)
  local copies, waits for them, and re-layouts  12.8 us (8%)
  between operations  6.22 us (4%)
  starting transfers between devices  5.84 us (4%)
  other arithmetic  2.56 us (2%)
  waiting for transfers between devices  1.83 us (1%)
    pallas_call x1, Pallas kernels, train_call(): pl.pallas_call(functools.partial(train_kernel, blocks), out_shape=(jax.Sh...  128 us
    unnamed x19, local copies, waits for them, and re-layouts  3.38 us
  transfers between devices with their start and end apart: 3, of which 1 were waited for; matrix products, arithmetic and copies ran while one was open for 5% of the time, Pallas kernels for 0%

profile of v2, /device:TPU:166, one launch (start us, length us, event | category | flops | bytes accessed | tf_op | source)
XLA Modules:
  0.0 157.7 jit_solution(10086472866824314897)
XLA Ops:
  0.6 0.0 copy-start.3
  0.7 1.4 fusion.7
  3.4 0.8 dynamic_slice.67
  4.1 1.9 %collective-permute-start.2 = (f32[192]{0:T(256)S(1)}, f32[192]{0:T(256)S(1)}, u32[]{:S(2)}, u32[]{:S(2)}) collective-permute-start(f32[192]{0:T(256)S(1)} %dynamic_slice.67), channel_id=1, source_target_pairs={{0,2},{1,3},{2,4},{3,5},{4,6},{5,7},{6,8},{7,9},{8,10},{9,11},{10,... | collective-permute-start | bytes 2312 | tf_op jit(solution)/shard_map/ppermute | solution.py:493
  6.1 0.7 fusion.5
  6.7 0.1 broadcast_in_dim.75
  6.8 0.8 constant_dynamic-slice_fusion.1
  7.7 0.0 copy-start.2
  7.7 0.9 constant_dynamic-slice_fusion.3
  8.7 0.9 constant_dynamic-slice_fusion
  9.6 0.0 copy-start
  9.7 0.2 concatenate.13
  9.9 1.8 %collective-permute-start = (s32[4,8,1024]{2,1,0:T(8,128)S(1)}, s32[4,8,1024]{2,1,0:T(8,128)S(1)}, u32[]{:S(2)}, u32[]{:S(2)}) collective-permute-start(s32[4,8,1024]{2,1,0:T(8,128)S(1)} %concatenate.13), channel_id=1, source_target_pairs={{0,2},{2,0},{1,3},{3,1},{4,6},{6,4},{5,7},{7,5},{8,10},{10,8},{9,1... | collective-permute-start | bytes 393224 | tf_op jit(solution)/shard_map/ppermute | solution.py:458
  11.6 1.2 dynamic-slice_bitcast_fusion
  12.8 2.2 %collective-permute-start.1 = (f32[400,192]{1,0:T(8,128)S(1)}, f32[400,192]{1,0:T(8,128)S(1)}, u32[]{:S(2)}, u32[]{:S(2)}) collective-permute-start(f32[400,192]{1,0:T(8,128)S(1)} %dynamic-slice_bitcast_fusion), channel_id=1, source_target_pairs={{0,2},{1,3},{2,4},{3,5},{4,6},{5,7},{6,8},{7,9},{8,10},{9,11},{10,... | collective-permute-start | bytes 921608 | tf_op jit(solution)/shard_map/ppermute | solution.py:492
  15.0 0.0 copy-done.3
  15.0 0.6 fusion.6
  19.5 0.1 broadcast_in_dim.69
  19.7 0.9 slice.9
  20.7 0.7 pad.46.rel_end
  21.4 0.2 concatenate.12
  21.5 0.0 collective-permute-done.2
  21.6 0.0 copy-done.2
  21.6 0.1 fusion.3
  21.6 0.0 collective-permute-done
  21.7 0.0 copy-start.1
  21.7 0.6 copy.30
  22.4 1.8 %collective-permute-done.1 = f32[400,192]{1,0:T(8,128)S(1)} collective-permute-done((f32[400,192]{1,0:T(8,128)S(1)}, f32[400,192]{1,0:T(8,128)S(1)}, u32[]{:S(2)}, u32[]{:S(2)}) %collective-permute-start.1) | collective-permute-done | bytes 307232 | tf_op jit(solution)/shard_map/ppermute | solution.py:492
  24.2 0.0 copy-done
  24.2 1.8 %fusion.1.own = f32[400,1024]{1,0:T(8,128)} fusion(s32[]{:T(128)S(6)} %min.16, f32[400,192]{1,0:T(8,128)S(1)} %collective-permute-done.1, f32[400,1024]{1,0:T(8,128)S(1)} %bitcast.37, pred[1024]{0:T(1024)(128)(4,1)S(1)} %iota_compare_fusion), kind=kLoop, calls=%fused_computation.3 | loop fusion | flops 819200 | bytes 3585028 | tf_op jit(solution)/shard_map/jit(_where)/select_n | solution.py:501
  26.0 0.0 copy-done.1
  26.0 0.6 broadcast_in_dim.80.own_state
  26.6 128.4 %train.1 = (f32[400,512]{1,0:T(8,128)}, f32[1,512]{1,0:T(1,128)}) custom-call(s32[4,1024]{1,0:T(4,128)} %bitcast.43, s32[4,8,1024]{2,1,0:T(8,128)} %copy-done.1, f32[400,1024]{1,0:T(8,128)} %fusion.1.own, f32[8,1024]{1,0:T(8,128)} %broadcast_in_dim.80.own_state, f32[400,4131]{1,0:T(8,128)} %bitcast.45, f32[400,128]{1,0:T(8,128)} %pad.46.rel_end), custom_call_target="tpu_custom_call" | custom-call | flops 40000000000 | bytes 10000000 | tf_op jit(solution)/shard_map/train/pallas_call | solution.py:391
  155.0 0.0 copy-start.4
  155.0 2.1 %copy.37 = f32[512,400]{0,1:T(8,128)} copy(f32[512,400]{0,1:T(8,128)} %bitcast.38) | data formatting | bytes 1638400
  157.1 0.0 copy-done.4
  157.1 0.6 copy.38
  (30 shorter events, 0.3 us)
Async XLA Ops:
  0.6 14.3 %copy-start.3 = (s32[128]{0:T(128)S(1)}, s32[128]{0:T(128)}, u32[]{:S(2)}) copy-start(s32[128]{0:T(128)} %param.13) | copy-start | bytes 1540
  4.1 17.4 %collective-permute-start.2 = (f32[192]{0:T(256)S(1)}, f32[192]{0:T(256)S(1)}, u32[]{:S(2)}, u32[]{:S(2)}) collective-permute-start(f32[192]{0:T(256)S(1)} %dynamic_slice.67), channel_id=1, source_target_pairs={{0,2},{1,3},{2,4},{3,5},{4,6},{5,7},{6,8},{7,9},{8,10},{9,11},{10,... | collective-permute-start | bytes 2312 | tf_op jit(solution)/shard_map/ppermute | solution.py:493
  7.7 13.8 %copy-start.2 = (f32[1024]{0:T(1024)S(1)}, f32[1024]{0:T(1024)}, u32[]{:S(2)}) copy-start(f32[1024]{0:T(1024)} %param.11) | copy-start | bytes 12292
  9.6 14.5 %copy-start = (f32[1024,400]{0,1:T(8,128)S(1)}, f32[1024,400]{0,1:T(8,128)}, u32[]{:S(2)}) copy-start(f32[1024,400]{0,1:T(8,128)} %param.10) | copy-start | bytes 4915204
  9.9 11.8 %collective-permute-start = (s32[4,8,1024]{2,1,0:T(8,128)S(1)}, s32[4,8,1024]{2,1,0:T(8,128)S(1)}, u32[]{:S(2)}, u32[]{:S(2)}) collective-permute-start(s32[4,8,1024]{2,1,0:T(8,128)S(1)} %concatenate.13), channel_id=1, source_target_pairs={{0,2},{2,0},{1,3},{3,1},{4,6},{6,4},{5,7},{7,5},{8,10},{10,8},{9,1... | collective-permute-start | bytes 393224 | tf_op jit(solution)/shard_map/ppermute | solution.py:458
  12.8 11.4 %collective-permute-start.1 = (f32[400,192]{1,0:T(8,128)S(1)}, f32[400,192]{1,0:T(8,128)S(1)}, u32[]{:S(2)}, u32[]{:S(2)}) collective-permute-start(f32[400,192]{1,0:T(8,128)S(1)} %dynamic-slice_bitcast_fusion), channel_id=1, source_target_pairs={{0,2},{1,3},{2,4},{3,5},{4,6},{5,7},{6,8},{7,9},{8,10},{9,11},{10,... | collective-permute-start | bytes 921608 | tf_op jit(solution)/shard_map/ppermute | solution.py:492
  21.7 4.3 %copy-start.1 = (s32[4,8,1024]{2,1,0:T(8,128)}, s32[4,8,1024]{2,1,0:T(8,128)S(1)}, u32[]{:S(2)}) copy-start(s32[4,8,1024]{2,1,0:T(8,128)S(1)} %broadcast_select_fusion.idx) | copy-start | bytes 393220
  155.0 2.1 %copy-start.4 = (f32[1,512]{1,0:T(1,128)S(1)}, f32[1,512]{1,0:T(1,128)}, u32[]{:S(2)}) copy-start(f32[1,512]{1,0:T(1,128)} %get-tuple-element.5) | copy-start | bytes 6148

commit v3 on v2

--- a/solution.py
+++ b/solution.py
@@ -61,8 +61,7 @@
     sibling = (m2 + 1 - c, r)
     ahead = (lax.rem(b + 2, blocks), r)
     behind = (lax.rem(b + blocks - 2, blocks), r)
-    ahead_far = (lax.rem(b + 4, blocks), r)
-    behind_far = (lax.rem(b + blocks - 4, blocks), r)
+    across = (b, 1 - r)
     here = c == r
     mine = pl.ds(pl.multiple_of(c * HALF, HALF), HALF)
     theirs = pl.ds(pl.multiple_of((1 - c) * HALF, HALF), HALF)
@@ -101,17 +100,18 @@
     def _():
         pl.semaphore_signal(barrier, inc=1, device_id=origin(0), device_id_type=MESH)
 
-    @pl.when(r == 0)
-    def _():
-        pl.semaphore_signal(barrier, inc=1, device_id=behind_far, device_id_type=MESH)
-
-    pl.semaphore_wait(barrier, STEPS + 3 - r - here.astype(jnp.int32))
+    @pl.when(r + c == 0)
+    def _():
+        pl.semaphore_signal(barrier, inc=1, device_id=across, device_id_type=MESH)
+
+    pl.semaphore_wait(barrier, STEPS + 2 - here.astype(jnp.int32) + r * (1 - c))
 
     share = remote(tab.at[0], tab.at[1], tab_send.at[0], tab_recv.at[0], sibling)
     share_state = remote(st.at[0], st.at[1], tab_send.at[1], tab_recv.at[1], sibling)
     onward = remote(tab.at[0], tab.at[2], tab_send.at[2], tab_recv.at[2], ahead)
+    relay = remote(tab.at[2], tab.at[2], tab_send.at[6], tab_recv.at[2], across)
     share_on = remote(tab.at[2], tab.at[3], tab_send.at[3], tab_recv.at[3], sibling)
-    far = remote(tab.at[1 - c, :, mine], tab.at[4, :, mine], tab_send.at[4], tab_recv.at[4], ahead_far)
+    far = remote(tab.at[3 - c, :, mine], tab.at[4, :, mine], tab_send.at[4], tab_recv.at[4], ahead)
     share_far = remote(tab.at[4, :, mine], tab.at[4, :, mine], tab_send.at[5], tab_recv.at[5], sibling)
     share_far_in = remote(tab.at[4, :, theirs], tab.at[4, :, theirs], tab_send.at[5], tab_recv.at[5], sibling)
 
@@ -136,7 +136,7 @@
     share.start()
     share_state.start()
 
-    @pl.when(c == 1)
+    @pl.when(jnp.logical_not(here))
     def _():
         onward.start()
 
@@ -167,10 +167,6 @@
     gather(0)
     share.wait_recv()
     share_state.wait_recv()
-
-    @pl.when(r == 0)
-    def _():
-        far.start()
 
     state[...] = jnp.where(here, st[0], st[1])
     for c0 in range(0, CAP, 256):
@@ -224,7 +220,7 @@
             dn_s[:, col] = (jax.nn.sigmoid(scores) * (live * (1.0 / N))).astype(BF)
         split_to(gdhl, pl.ds(E, N), dot(qb_s[...], dn_s[...], NT))
 
-        @pl.when(jnp.logical_and(s == 0, c == 0))
+        @pl.when(jnp.logical_and(s == 0, r + c == 2))
         def _():
             onward.start()
 
@@ -273,27 +269,22 @@
             gl_copy(s, 1).start()
             gather(s + 1)
 
-        @pl.when(s == 0)
-        def _():
-            @pl.when(c == 0)
-            def _():
-                share_on.wait_recv()
-
-            @pl.when(c == 1)
-            def _():
-                onward.wait_recv()
-                share_on.start()
-
-        @pl.when(s == 1)
-        def _():
-            @pl.when(c == 0)
-            def _():
-                onward.wait_recv()
-                share_on.start()
-
-            @pl.when(c == 1)
-            def _():
-                share_on.wait_recv()
+        @pl.when(jnp.logical_and(s == 0, here) | jnp.logical_and(s == 1, jnp.logical_not(here)))
+        def _():
+            share_on.wait_recv()
+
+        @pl.when(jnp.logical_and(s == 1, here) | jnp.logical_and(s == 0, jnp.logical_not(here)))
+        def _():
+            onward.wait_recv()
+            share_on.start()
+
+        @pl.when(jnp.logical_and(s == 0, r > c))
+        def _():
+            relay.start()
+
+        @pl.when(jnp.logical_and(s == 0, r == 0))
+        def _():
+            far.start()
 
         @pl.when(jnp.logical_and(s == 2, r == 0))
         def _():
@@ -358,8 +349,15 @@
 
     share.wait_send()
     share_state.wait_send()
-    onward.wait_send()
     share_on.wait_send()
+
+    @pl.when(r + c > 0)
+    def _():
+        onward.wait_send()
+
+    @pl.when(r > c)
+    def _():
+        relay.wait_send()
 
     @pl.when(r == 0)
     def _():
@@ -422,7 +420,7 @@
             pltpu.VMEM((2, D, HALF), F32),
             pltpu.VMEM((2, 8, HALF), F32),
             dma((6,)),
-            dma((6,)),
+            dma((7,)),
             dma((6,)),
             dma((2, 2)),
             dma((2, 2)),

time: 158 us -> 156 us (0.987)
  the two profiles are of different devices: /device:TPU:166 before, /device:TPU:27 now
where the time goes in v3:
time: 156 us; the launch traced here: 153 us
  Pallas kernels  124 us (79%)
  local copies, waits for them, and re-layouts  13.1 us (8%)
  starting transfers between devices  7.16 us (5%)
  between operations  6.23 us (4%)
  other arithmetic  2.57 us (2%)
    pallas_call x1, Pallas kernels, train_call(): pl.pallas_call(functools.partial(train_kernel, blocks), out_shape=(jax.Sh...  124 us
    ppermute x1, starting transfers between devices, local(): low_s = lax.ppermute(low_s, BOTH, shift)  3.72 us
    unnamed x19, local copies, waits for them, and re-layouts  3.38 us
    ppermute x1, starting transfers between devices, local(): low_t = lax.ppermute(low_t, BOTH, shift)  3.34 us
  transfers between devices with their start and end apart: 3, of which 0 were waited for; matrix products, arithmetic and copies ran while one was open for 5% of the time, Pallas kernels for 0%

profile of v3, /device:TPU:27, one launch (start us, length us, event | category | flops | bytes accessed | tf_op | source)
XLA Modules:
  0.0 153.4 jit_solution(17862420899904652611)
XLA Ops:
  0.6 0.0 copy-start.3
  0.7 1.4 fusion.7
  3.4 0.8 dynamic_slice.67
  4.1 3.7 %collective-permute-start.2 = (f32[192]{0:T(256)S(1)}, f32[192]{0:T(256)S(1)}, u32[]{:S(2)}, u32[]{:S(2)}) collective-permute-start(f32[192]{0:T(256)S(1)} %dynamic_slice.67), channel_id=1, source_target_pairs={{0,2},{1,3},{2,4},{3,5},{4,6},{5,7},{6,8},{7,9},{8,10},{9,11},{10,... | collective-permute-start | bytes 2312 | tf_op jit(solution)/shard_map/ppermute | solution.py:491
  7.9 0.7 fusion.5
  8.5 0.1 broadcast_in_dim.75
  8.7 0.8 constant_dynamic-slice_fusion.1
  9.5 0.0 copy-start.2
  9.5 0.9 constant_dynamic-slice_fusion.3
  10.5 0.9 constant_dynamic-slice_fusion
  11.5 0.0 copy-start
  11.5 0.2 concatenate.13
  11.7 0.1 collective-permute-start
  11.8 1.4 dynamic-slice_bitcast_fusion
  13.2 3.3 %collective-permute-start.1 = (f32[400,192]{1,0:T(8,128)S(1)}, f32[400,192]{1,0:T(8,128)S(1)}, u32[]{:S(2)}, u32[]{:S(2)}) collective-permute-start(f32[400,192]{1,0:T(8,128)S(1)} %dynamic-slice_bitcast_fusion), channel_id=1, source_target_pairs={{0,2},{1,3},{2,4},{3,5},{4,6},{5,7},{6,8},{7,9},{8,10},{9,11},{10,... | collective-permute-start | bytes 921608 | tf_op jit(solution)/shard_map/ppermute | solution.py:490
  16.5 0.0 copy-done.3
  16.6 0.6 fusion.6
  21.0 0.1 broadcast_in_dim.69
  21.3 0.9 slice.9
  22.3 0.7 pad.46.rel_end
  23.0 0.2 concatenate.12
  23.1 0.0 collective-permute-done.2
  23.1 0.0 copy-done.2
  23.1 0.1 fusion.3
  23.2 0.0 collective-permute-done
  23.2 0.0 copy-start.1
  23.3 0.6 copy.30
  23.9 0.0 collective-permute-done.1
  23.9 0.0 copy-done
  23.9 1.8 %fusion.1.own = f32[400,1024]{1,0:T(8,128)} fusion(s32[]{:T(128)S(6)} %min.16, f32[400,192]{1,0:T(8,128)S(1)} %collective-permute-done.1, f32[400,1024]{1,0:T(8,128)S(1)} %bitcast.37, pred[1024]{0:T(1024)(128)(4,1)S(1)} %iota_compare_fusion), kind=kLoop, calls=%fused_computation.3 | loop fusion | flops 819200 | bytes 3585028 | tf_op jit(solution)/shard_map/jit(_where)/select_n | solution.py:499
  25.7 0.0 copy-done.1
  25.7 0.6 broadcast_in_dim.80.own_state
  26.4 124.4 %train.1 = (f32[400,512]{1,0:T(8,128)}, f32[1,512]{1,0:T(1,128)}) custom-call(s32[4,1024]{1,0:T(4,128)} %bitcast.43, s32[4,8,1024]{2,1,0:T(8,128)} %copy-done.1, f32[400,1024]{1,0:T(8,128)} %fusion.1.own, f32[8,1024]{1,0:T(8,128)} %broadcast_in_dim.80.own_state, f32[400,4131]{1,0:T(8,128)} %bitcast.45, f32[400,128]{1,0:T(8,128)} %pad.46.rel_end), custom_call_target="tpu_custom_call" | custom-call | flops 40000000000 | bytes 10000000 | tf_op jit(solution)/shard_map/train/pallas_call | solution.py:389
  150.7 0.0 copy-start.4
  150.7 2.1 %copy.37 = f32[512,400]{0,1:T(8,128)} copy(f32[512,400]{0,1:T(8,128)} %bitcast.38) | data formatting | bytes 1638400
  152.8 0.0 copy-done.4
  152.8 0.6 copy.38
  (30 shorter events, 0.3 us)
Async XLA Ops:
  0.6 15.9 %copy-start.3 = (s32[128]{0:T(128)S(1)}, s32[128]{0:T(128)}, u32[]{:S(2)}) copy-start(s32[128]{0:T(128)} %param.13) | copy-start | bytes 1540
  4.1 19.0 %collective-permute-start.2 = (f32[192]{0:T(256)S(1)}, f32[192]{0:T(256)S(1)}, u32[]{:S(2)}, u32[]{:S(2)}) collective-permute-start(f32[192]{0:T(256)S(1)} %dynamic_slice.67), channel_id=1, source_target_pairs={{0,2},{1,3},{2,4},{3,5},{4,6},{5,7},{6,8},{7,9},{8,10},{9,11},{10,... | collective-permute-start | bytes 2312 | tf_op jit(solution)/shard_map/ppermute | solution.py:491
  9.5 13.6 %copy-start.2 = (f32[1024]{0:T(1024)S(1)}, f32[1024]{0:T(1024)}, u32[]{:S(2)}) copy-start(f32[1024]{0:T(1024)} %param.11) | copy-start | bytes 12292
  11.5 12.5 %copy-start = (f32[1024,400]{0,1:T(8,128)S(1)}, f32[1024,400]{0,1:T(8,128)}, u32[]{:S(2)}) copy-start(f32[1024,400]{0,1:T(8,128)} %param.10) | copy-start | bytes 4915204
  11.7 11.5 %collective-permute-start = (s32[4,8,1024]{2,1,0:T(8,128)S(1)}, s32[4,8,1024]{2,1,0:T(8,128)S(1)}, u32[]{:S(2)}, u32[]{:S(2)}) collective-permute-start(s32[4,8,1024]{2,1,0:T(8,128)S(1)} %concatenate.13), channel_id=1, source_target_pairs={{0,2},{2,0},{1,3},{3,1},{4,6},{6,4},{5,7},{7,5},{8,10},{10,8},{9,1... | collective-permute-start | bytes 393224 | tf_op jit(solution)/shard_map/ppermute | solution.py:456
  13.2 10.7 %collective-permute-start.1 = (f32[400,192]{1,0:T(8,128)S(1)}, f32[400,192]{1,0:T(8,128)S(1)}, u32[]{:S(2)}, u32[]{:S(2)}) collective-permute-start(f32[400,192]{1,0:T(8,128)S(1)} %dynamic-slice_bitcast_fusion), channel_id=1, source_target_pairs={{0,2},{1,3},{2,4},{3,5},{4,6},{5,7},{6,8},{7,9},{8,10},{9,11},{10,... | collective-permute-start | bytes 921608 | tf_op jit(solution)/shard_map/ppermute | solution.py:490
  23.2 2.5 %copy-start.1 = (s32[4,8,1024]{2,1,0:T(8,128)}, s32[4,8,1024]{2,1,0:T(8,128)S(1)}, u32[]{:S(2)}) copy-start(s32[4,8,1024]{2,1,0:T(8,128)S(1)} %broadcast_select_fusion.idx) | copy-start | bytes 393220
  150.7 2.1 %copy-start.4 = (f32[1,512]{1,0:T(1,128)S(1)}, f32[1,512]{1,0:T(1,128)}, u32[]{:S(2)}) copy-start(f32[1,512]{1,0:T(1,128)} %get-tuple-element.5) | copy-start | bytes 6148

commit v4 on v3

--- a/solution.py
+++ b/solution.py
@@ -108,12 +108,13 @@
 
     share = remote(tab.at[0], tab.at[1], tab_send.at[0], tab_recv.at[0], sibling)
     share_state = remote(st.at[0], st.at[1], tab_send.at[1], tab_recv.at[1], sibling)
-    onward = remote(tab.at[0], tab.at[2], tab_send.at[2], tab_recv.at[2], ahead)
-    relay = remote(tab.at[2], tab.at[2], tab_send.at[6], tab_recv.at[2], across)
-    share_on = remote(tab.at[2], tab.at[3], tab_send.at[3], tab_recv.at[3], sibling)
-    far = remote(tab.at[3 - c, :, mine], tab.at[4, :, mine], tab_send.at[4], tab_recv.at[4], ahead)
-    share_far = remote(tab.at[4, :, mine], tab.at[4, :, mine], tab_send.at[5], tab_recv.at[5], sibling)
-    share_far_in = remote(tab.at[4, :, theirs], tab.at[4, :, theirs], tab_send.at[5], tab_recv.at[5], sibling)
+    t1 = remote(tab.at[0], tab.at[2], tab_send.at[2], tab_recv.at[2], ahead)
+    t2a = remote(tab.at[0, :, 0:HALF], tab.at[2, :, 0:HALF], tab_send.at[3], tab_recv.at[3], ahead)
+    t2b = remote(tab.at[0, :, HALF:], tab.at[2, :, HALF:], tab_send.at[4], tab_recv.at[4], ahead)
+    relay = remote(tab.at[2, :, HALF:], tab.at[2, :, HALF:], tab_send.at[5], tab_recv.at[5], across)
+    t3 = remote(tab.at[2], tab.at[4], tab_send.at[6], tab_recv.at[6], ahead)
+    share_on = remote(tab.at[2], tab.at[3], tab_send.at[7], tab_recv.at[7], sibling)
+    share_far = remote(tab.at[4], tab.at[4], tab_send.at[8], tab_recv.at[8], sibling)
 
     def gl_copy(s, k):
         p = lax.rem(s, 2)
@@ -136,9 +137,13 @@
     share.start()
     share_state.start()
 
-    @pl.when(jnp.logical_not(here))
-    def _():
-        onward.start()
+    @pl.when(r < c)
+    def _():
+        t1.start()
+
+    @pl.when(r > c)
+    def _():
+        t2b.start()
 
     for k in range(full):
         get_rel(k).wait()
@@ -167,6 +172,11 @@
     gather(0)
     share.wait_recv()
     share_state.wait_recv()
+
+    @pl.when(r + c == 2)
+    def _():
+        t1.start()
+
 
     state[...] = jnp.where(here, st[0], st[1])
     for c0 in range(0, CAP, 256):
@@ -220,9 +230,14 @@
             dn_s[:, col] = (jax.nn.sigmoid(scores) * (live * (1.0 / N))).astype(BF)
         split_to(gdhl, pl.ds(E, N), dot(qb_s[...], dn_s[...], NT))
 
-        @pl.when(jnp.logical_and(s == 0, r + c == 2))
-        def _():
-            onward.start()
+        @pl.when(jnp.logical_and(s == 0, r + c == 0))
+        def _():
+            t2a.start()
+
+        @pl.when(jnp.logical_and(s == 0, r > c))
+        def _():
+            t2b.wait_recv()
+            relay.start()
 
         def right_half(part):
             y = dot(gdhl[...], oht[part, :], NT)
@@ -267,30 +282,46 @@
         @pl.when(s < STEPS - 1)
         def _():
             gl_copy(s, 1).start()
+
+        @pl.when(jnp.logical_and(s == r, c == 1))
+        def _():
+            t1.wait_recv()
+            share_on.start()
+
+        @pl.when(jnp.logical_and(s == r + 1, c == 0))
+        def _():
+            t2a.wait_recv()
+
+            @pl.when(r == 0)
+            def _():
+                relay.wait_recv()
+
+            share_on.start()
+
+        @pl.when(jnp.logical_and(s == 0, r > c))
+        def _():
+            t2a.start()
+
+        @pl.when(jnp.logical_and(s == 2, r < c))
+        def _():
+            t3.wait_recv()
+            share_far.start()
+
+        @pl.when(s < STEPS - 1)
+        def _():
             gather(s + 1)
 
-        @pl.when(jnp.logical_and(s == 0, here) | jnp.logical_and(s == 1, jnp.logical_not(here)))
+        @pl.when(jnp.logical_and(s == 0, r < c))
+        def _():
+            t3.start()
+
+        @pl.when(s == r + c)
         def _():
             share_on.wait_recv()
 
-        @pl.when(jnp.logical_and(s == 1, here) | jnp.logical_and(s == 0, jnp.logical_not(here)))
-        def _():
-            onward.wait_recv()
-            share_on.start()
-
-        @pl.when(jnp.logical_and(s == 0, r > c))
-        def _():
-            relay.start()
-
-        @pl.when(jnp.logical_and(s == 0, r == 0))
-        def _():
-            far.start()
-
-        @pl.when(jnp.logical_and(s == 2, r == 0))
-        def _():
-            far.wait_recv()
-            share_far.start()
-            share_far_in.wait_recv()
+        @pl.when(jnp.logical_and(s == 2, r + c == 0))
+        def _():
+            share_far.wait_recv()
 
         @pl.when(jnp.logical_and(s == 1, here))
         def _():
@@ -351,17 +382,22 @@
     share_state.wait_send()
     share_on.wait_send()
 
-    @pl.when(r + c > 0)
-    def _():
-        onward.wait_send()
+    @pl.when(c == 1)
+    def _():
+        t1.wait_send()
+
+    @pl.when(c == 0)
+    def _():
+        t2a.wait_send()
 
     @pl.when(r > c)
     def _():
+        t2b.wait_send()
         relay.wait_send()
 
-    @pl.when(r == 0)
-    def _():
-        far.wait_send()
+    @pl.when(r < c)
+    def _():
+        t3.wait_send()
         share_far.wait_send()
 
     for s in range(1, STEPS):
@@ -420,8 +456,8 @@
             pltpu.VMEM((2, D, HALF), F32),
             pltpu.VMEM((2, 8, HALF), F32),
             dma((6,)),
-            dma((7,)),
-            dma((6,)),
+            dma((9,)),
+            dma((9,)),
             dma((2, 2)),
             dma((2, 2)),
             dma((2,)),

time: 156 us -> 142 us (0.910)
  Pallas kernels: 124 us -> 110 us
    pallas_call x1, Pallas kernels: 124 us -> 110 us  [train_call(): pl.pallas_call(functools.partial(train_kernel, blocks), out_shape=(jax.Sh...]
  transfers between devices with their start and end apart: 3 -> 3, of which waited for: 0 -> 0; matrix products, arithmetic and copies ran while one was open for 5% -> 6% of each run, Pallas kernels for 0% -> 0%
where the time goes in v4:
time: 142 us; the launch traced here: 139 us
  Pallas kernels  110 us (77%)
  local copies, waits for them, and re-layouts  13 us (9%)
  starting transfers between devices  7.23 us (5%)
  between operations  6.23 us (4%)
  other arithmetic  2.57 us (2%)
    pallas_call x1, Pallas kernels, train_call(): pl.pallas_call(functools.partial(train_kernel, blocks), out_shape=(jax.Sh...  110 us
    ppermute x1, starting transfers between devices, local(): low_s = lax.ppermute(low_s, BOTH, shift)  3.72 us
    ppermute x1, starting transfers between devices, local(): low_t = lax.ppermute(low_t, BOTH, shift)  3.42 us
    unnamed x19, local copies, waits for them, and re-layouts  3.38 us
  transfers between devices with their start and end apart: 3, of which 0 were waited for; matrix products, arithmetic and copies ran while one was open for 6% of the time, Pallas kernels for 0%

profile of v4, /device:TPU:27, one launch (start us, length us, event | category | flops | bytes accessed | tf_op | source)
XLA Modules:
  0.0 139.4 jit_solution(5631162335548249910)
XLA Ops:
  0.6 0.0 copy-start.3
  0.7 1.4 fusion.7
  3.4 0.8 dynamic_slice.67
  4.1 3.7 %collective-permute-start.2 = (f32[192]{0:T(256)S(1)}, f32[192]{0:T(256)S(1)}, u32[]{:S(2)}, u32[]{:S(2)}) collective-permute-start(f32[192]{0:T(256)S(1)} %dynamic_slice.67), channel_id=1, source_target_pairs={{0,2},{1,3},{2,4},{3,5},{4,6},{5,7},{6,8},{7,9},{8,10},{9,11},{10,... | collective-permute-start | bytes 2312 | tf_op jit(solution)/shard_map/ppermute | solution.py:527
  7.9 0.7 fusion.5
  8.5 0.1 broadcast_in_dim.75
  8.7 0.8 constant_dynamic-slice_fusion.1
  9.5 0.0 copy-start.2
  9.5 0.9 constant_dynamic-slice_fusion.3
  10.5 0.9 constant_dynamic-slice_fusion
  11.5 0.0 copy-start
  11.5 0.2 concatenate.13
  11.7 0.1 collective-permute-start
  11.8 1.3 dynamic-slice_bitcast_fusion
  13.1 3.4 %collective-permute-start.1 = (f32[400,192]{1,0:T(8,128)S(1)}, f32[400,192]{1,0:T(8,128)S(1)}, u32[]{:S(2)}, u32[]{:S(2)}) collective-permute-start(f32[400,192]{1,0:T(8,128)S(1)} %dynamic-slice_bitcast_fusion), channel_id=1, source_target_pairs={{0,2},{1,3},{2,4},{3,5},{4,6},{5,7},{6,8},{7,9},{8,10},{9,11},{10,... | collective-permute-start | bytes 921608 | tf_op jit(solution)/shard_map/ppermute | solution.py:526
  16.5 0.0 copy-done.3
  16.6 0.6 fusion.6
  21.0 0.1 broadcast_in_dim.69
  21.3 0.9 slice.9
  22.3 0.7 pad.46.rel_end
  23.0 0.2 concatenate.12
  23.1 0.0 collective-permute-done.2
  23.1 0.0 copy-done.2
  23.1 0.1 fusion.3
  23.2 0.0 collective-permute-done
  23.2 0.0 copy-start.1
  23.3 0.6 copy.30
  23.9 0.0 collective-permute-done.1
  23.9 0.0 copy-done
  23.9 1.8 %fusion.1.own = f32[400,1024]{1,0:T(8,128)} fusion(s32[]{:T(128)S(6)} %min.16, f32[400,192]{1,0:T(8,128)S(1)} %collective-permute-done.1, f32[400,1024]{1,0:T(8,128)S(1)} %bitcast.37, pred[1024]{0:T(1024)(128)(4,1)S(1)} %iota_compare_fusion), kind=kLoop, calls=%fused_computation.3 | loop fusion | flops 819200 | bytes 3585028 | tf_op jit(solution)/shard_map/jit(_where)/select_n | solution.py:535
  25.7 0.0 copy-done.1
  25.7 0.6 broadcast_in_dim.80.own_state
  26.4 110.4 %train.1 = (f32[400,512]{1,0:T(8,128)}, f32[1,512]{1,0:T(1,128)}) custom-call(s32[4,1024]{1,0:T(4,128)} %bitcast.43, s32[4,8,1024]{2,1,0:T(8,128)} %copy-done.1, f32[400,1024]{1,0:T(8,128)} %fusion.1.own, f32[8,1024]{1,0:T(8,128)} %broadcast_in_dim.80.own_state, f32[400,4131]{1,0:T(8,128)} %bitcast.45, f32[400,128]{1,0:T(8,128)} %pad.46.rel_end), custom_call_target="tpu_custom_call" | custom-call | flops 40000000000 | bytes 10000000 | tf_op jit(solution)/shard_map/train/pallas_call | solution.py:425
  136.7 0.0 copy-start.4
  136.7 2.1 %copy.37 = f32[512,400]{0,1:T(8,128)} copy(f32[512,400]{0,1:T(8,128)} %bitcast.38) | data formatting | bytes 1638400
  138.8 0.0 copy-done.4
  138.8 0.6 copy.38
  (30 shorter events, 0.3 us)
Async XLA Ops:
  0.6 15.9 %copy-start.3 = (s32[128]{0:T(128)S(1)}, s32[128]{0:T(128)}, u32[]{:S(2)}) copy-start(s32[128]{0:T(128)} %param.13) | copy-start | bytes 1540
  4.1 19.0 %collective-permute-start.2 = (f32[192]{0:T(256)S(1)}, f32[192]{0:T(256)S(1)}, u32[]{:S(2)}, u32[]{:S(2)}) collective-permute-start(f32[192]{0:T(256)S(1)} %dynamic_slice.67), channel_id=1, source_target_pairs={{0,2},{1,3},{2,4},{3,5},{4,6},{5,7},{6,8},{7,9},{8,10},{9,11},{10,... | collective-permute-start | bytes 2312 | tf_op jit(solution)/shard_map/ppermute | solution.py:527
  9.5 13.6 %copy-start.2 = (f32[1024]{0:T(1024)S(1)}, f32[1024]{0:T(1024)}, u32[]{:S(2)}) copy-start(f32[1024]{0:T(1024)} %param.11) | copy-start | bytes 12292
  11.5 12.5 %copy-start = (f32[1024,400]{0,1:T(8,128)S(1)}, f32[1024,400]{0,1:T(8,128)}, u32[]{:S(2)}) copy-start(f32[1024,400]{0,1:T(8,128)} %param.10) | copy-start | bytes 4915204
  11.7 11.5 %collective-permute-start = (s32[4,8,1024]{2,1,0:T(8,128)S(1)}, s32[4,8,1024]{2,1,0:T(8,128)S(1)}, u32[]{:S(2)}, u32[]{:S(2)}) collective-permute-start(s32[4,8,1024]{2,1,0:T(8,128)S(1)} %concatenate.13), channel_id=1, source_target_pairs={{0,2},{2,0},{1,3},{3,1},{4,6},{6,4},{5,7},{7,5},{8,10},{10,8},{9,1... | collective-permute-start | bytes 393224 | tf_op jit(solution)/shard_map/ppermute | solution.py:492
  13.1 10.8 %collective-permute-start.1 = (f32[400,192]{1,0:T(8,128)S(1)}, f32[400,192]{1,0:T(8,128)S(1)}, u32[]{:S(2)}, u32[]{:S(2)}) collective-permute-start(f32[400,192]{1,0:T(8,128)S(1)} %dynamic-slice_bitcast_fusion), channel_id=1, source_target_pairs={{0,2},{1,3},{2,4},{3,5},{4,6},{5,7},{6,8},{7,9},{8,10},{9,11},{10,... | collective-permute-start | bytes 921608 | tf_op jit(solution)/shard_map/ppermute | solution.py:526
  23.2 2.5 %copy-start.1 = (s32[4,8,1024]{2,1,0:T(8,128)}, s32[4,8,1024]{2,1,0:T(8,128)S(1)}, u32[]{:S(2)}) copy-start(s32[4,8,1024]{2,1,0:T(8,128)S(1)} %broadcast_select_fusion.idx) | copy-start | bytes 393220
  136.7 2.1 %copy-start.4 = (f32[1,512]{1,0:T(1,128)S(1)}, f32[1,512]{1,0:T(1,128)}, u32[]{:S(2)}) copy-start(f32[1,512]{1,0:T(1,128)} %get-tuple-element.5) | copy-start | bytes 6148

commit v5 on v4

--- a/solution.py
+++ b/solution.py
@@ -18,8 +18,7 @@
 E = 1024
 N = 512
 CH = 512
-LOW = 192
-OLD_CAP = 2048
+LOW = 256
 ENTITIES = 122880
 STEPS = 4
 MESH = pl.DeviceIdType.MESH
@@ -49,11 +48,11 @@
         device_id_type=MESH)
 
 
-def train_kernel(blocks, ids, idx, own, own_state, rel, rel_end, out, out_state,
-                 tab, st, rel_s, rel_t, rows, left, state, lhl, rhl, ohs, oht, gshl, gdhl,
+def train_kernel(blocks, ids, old, new, idx, saved, saved_state, rel, rel_end, out, out_state,
+                 low_out, low_in, tab, st, rel_s, rel_t, rows, left, state, lhl, rhl, ohs, oht, gshl, gdhl,
                  q_s, g_s, d_s, dp_s, qb_s, dn_s, glo, gli, gro, gri, gsum, carr, lfin, sfin,
                  local_sem, tab_send, tab_recv, gl_send, gl_recv, gr_send, gr_recv,
-                 home_send, home_recv, fin_send, fin_recv):
+                 home_send, home_recv, fin_send, fin_recv, low_send, low_recv):
     b = lax.axis_index("blk")
     r = lax.axis_index("rep")
     c = lax.rem(b, 2)
@@ -62,6 +61,8 @@
     ahead = (lax.rem(b + 2, blocks), r)
     behind = (lax.rem(b + blocks - 2, blocks), r)
     across = (b, 1 - r)
+    following = (lax.rem(b + 1, blocks), r)
+    previous = (lax.rem(b + blocks - 1, blocks), r)
     here = c == r
     mine = pl.ds(pl.multiple_of(c * HALF, HALF), HALF)
     theirs = pl.ds(pl.multiple_of((1 - c) * HALF, HALF), HALF)
@@ -82,14 +83,13 @@
         return pltpu.make_async_copy(
             rel.at[:, k * CAP : (k + 1) * CAP], glo.at[k % 2], local_sem.at[4 + k % 2])
 
-    get_own = pltpu.make_async_copy(own, tab.at[0], local_sem.at[1])
-    get_state = pltpu.make_async_copy(own_state, st.at[0], local_sem.at[2])
+    get_own = pltpu.make_async_copy(saved, tab.at[0], local_sem.at[1])
     get_own.start()
-    get_state.start()
     for k in range(min(2, full)):
         get_rel(k).start()
     get_rel(full).start()
 
+    low_in[...] = jnp.zeros_like(low_in)
     barrier = pltpu.get_barrier_semaphore()
     pl.semaphore_signal(barrier, inc=1, device_id=sibling, device_id_type=MESH)
     pl.semaphore_signal(barrier, inc=1, device_id=behind, device_id_type=MESH)
@@ -104,7 +104,32 @@
     def _():
         pl.semaphore_signal(barrier, inc=1, device_id=across, device_id_type=MESH)
 
-    pl.semaphore_wait(barrier, STEPS + 2 - here.astype(jnp.int32) + r * (1 - c))
+    @pl.when(c == 0)
+    def _():
+        pl.semaphore_signal(barrier, inc=1, device_id=previous, device_id_type=MESH)
+
+    st[0] = jnp.broadcast_to(saved_state[...], (8, CAP))
+    nxt = lax.div(jnp.minimum(b + 1, blocks - 1), 2)
+    even_end = old[nxt] - old[jnp.maximum(nxt - 1, 0)] - CAP
+    cut = jnp.where(c == 0, CAP, even_end)
+    shift = lax.rem(CAP + LOW - cut, CAP)
+    get_own.wait()
+    for at in range(0, D, 80):
+        x = tab[0, at : at + 80, :]
+        low_out[at : at + 80, :] = pltpu.roll(x, shift, 1)[:, 0:LOW]
+    low_out[D : D + 8, :] = pltpu.roll(st[0], shift, 1)[:, 0:LOW]
+    low = remote(low_out, low_in, low_send.at[0], low_recv.at[0], following)
+    low_end = remote(low_out.at[:, LOW // 2 :], low_in.at[:, LOW // 2 :], low_send.at[0], low_recv.at[0], following)
+
+    pl.semaphore_wait(barrier, STEPS + 2 - here.astype(jnp.int32) + r * (1 - c) + c)
+
+    @pl.when(c == 0)
+    def _():
+        low.start()
+
+    @pl.when(c == 1)
+    def _():
+        low_end.start()
 
     share = remote(tab.at[0], tab.at[1], tab_send.at[0], tab_recv.at[0], sibling)
     share_state = remote(st.at[0], st.at[1], tab_send.at[1], tab_recv.at[1], sibling)
@@ -132,20 +157,7 @@
     def home_local(s):
         return pltpu.make_async_copy(gsum.at[0], carr.at[0], local_sem.at[3])
 
-    get_own.wait()
-    get_state.wait()
-    share.start()
-    share_state.start()
-
-    @pl.when(r < c)
-    def _():
-        t1.start()
-
-    @pl.when(r > c)
-    def _():
-        t2b.start()
-
-    for k in range(full):
+    def turn_block(k):
         get_rel(k).wait()
 
         def turn(i, carry):
@@ -156,6 +168,47 @@
         lax.fori_loop(0, CAP // 128, turn, 0)
         if k + 2 < full:
             get_rel(k + 2).start()
+
+    for k in range(min(2, full)):
+        turn_block(k)
+
+    @pl.when(c == 1)
+    def _():
+        low.wait_recv()
+
+    @pl.when(c == 0)
+    def _():
+        low_end.wait_recv()
+
+    first = new[b]
+    start = old[lax.div(b, 2)]
+    end = jnp.where(b + 1 < blocks, new[jnp.minimum(b + 1, blocks - 1)], ENTITIES)
+    taken = jnp.where(c == 1, CAP - (first - start), start - first)
+    lane = lax.broadcasted_iota(jnp.int32, (8, CAP), 1)
+
+    def restored(x, tail, fill):
+        y = pltpu.roll(x, taken, 1)
+        front = pltpu.roll(tail, taken, 1)
+        front = jnp.where(lane[:, 0:LOW] < taken, front, y[:, 0:LOW])
+        y = jnp.concatenate([front, y[:, LOW:]], axis=1)
+        return jnp.where(lane < end - first, y, fill)
+
+    for at in range(0, D, 8):
+        tab[0, at : at + 8, :] = restored(tab[0, at : at + 8, :], low_in[at : at + 8, :], 0.0)
+    st[0] = restored(st[0], low_in[D : D + 8, :], 1.0)
+    share.start()
+    share_state.start()
+
+    @pl.when(r < c)
+    def _():
+        t1.start()
+
+    @pl.when(r > c)
+    def _():
+        t2b.start()
+
+    for k in range(min(2, full), full):
+        turn_block(k)
     get_rel(full).wait()
     rel_s[full * CAP :, :] = gro[0, :, 0:128].T[0 : rel.shape[1] - full * CAP]
 
@@ -382,8 +435,13 @@
     share_state.wait_send()
     share_on.wait_send()
 
+    @pl.when(c == 0)
+    def _():
+        low.wait_send()
+
     @pl.when(c == 1)
     def _():
+        low_end.wait_send()
         t1.wait_send()
 
     @pl.when(c == 0)
@@ -420,14 +478,16 @@
     home_copy(STEPS - 1).wait_send()
 
 
-def train_call(blocks, ids, idx, own, own_state, rel, rel_end):
+def train_call(blocks, ids, old, new, idx, saved, saved_state, rel, rel_end):
     dma = pltpu.SemaphoreType.DMA
     return pl.pallas_call(
         functools.partial(train_kernel, blocks),
         out_shape=(jax.ShapeDtypeStruct((D, HALF), F32), jax.ShapeDtypeStruct((1, HALF), F32)),
-        in_specs=[SMEM, VMEM, ANY, ANY, ANY, ANY],
+        in_specs=[SMEM, SMEM, SMEM, VMEM, ANY, VMEM, ANY, ANY],
         out_specs=(VMEM, VMEM),
         scratch_shapes=[
+            pltpu.VMEM((D + 8, LOW), F32),
+            pltpu.VMEM((D + 8, LOW), F32),
             pltpu.VMEM((5, D, CAP), F32),
             pltpu.VMEM((2, 8, CAP), F32),
             pltpu.VMEM(rel.shape[::-1], F32),
@@ -466,12 +526,14 @@
             dma((STEPS,)),
             dma((2,)),
             dma((2,)),
+            dma((1,)),
+            dma((1,)),
         ],
         compiler_params=pltpu.CompilerParams(
             vmem_limit_bytes=VMEM_LIMIT, collective_id=0, has_side_effects=True),
         cost_estimate=pl.CostEstimate(flops=4 * 10**10, bytes_accessed=10**7, transcendentals=0),
         name="train",
-    )(ids, idx, own, own_state, rel, rel_end)
+    )(ids, old, new, idx, saved, saved_state, rel, rel_end)
 
 
 def local(blocks, saved_rows, saved_state, old_starts, new_starts, relations,
@@ -510,37 +572,11 @@
     theirs = sibling(pack(1 - c))
     idx = jnp.where(c == r, pack(c), theirs)
 
-    table = saved_rows.T
-    last = old_starts.shape[0] - 1
-
-    def tail_end(q):
-        p = q // 2
-        even = old_starts[p] - old_starts[jnp.maximum(p - 1, 0)] - CAP
-        return jnp.where(q % 2 == 1, CAP, even)
-
-    nxt = jnp.minimum(b + 1, blocks - 1)
-    cut = jnp.clip(tail_end(nxt) - LOW, 0, CAP - LOW)
-    low_t = lax.dynamic_slice(table, (0, cut), (D, LOW))
-    low_s = lax.dynamic_slice(saved_state, (cut,), (LOW,))
-    shift = [(((q - 1) * 2 + rr), q * 2 + rr) for q in range(1, blocks) for rr in range(2)]
-    low_t = lax.ppermute(low_t, BOTH, shift)
-    low_s = lax.ppermute(low_s, BOTH, shift)
-    first = new_starts[b]
-    end = jnp.where(b + 1 < blocks, new_starts[nxt], ENTITIES)
-    p = jnp.minimum(b // 2, last)
-    k = jnp.where(b % 2 == 1, CAP - (first - old_starts[p]), old_starts[p] - first)
-    begin = jnp.clip(LOW - k, 0, LOW)
-    valid = jnp.arange(CAP, dtype=jnp.int32)[None] < end - first
-    own = lax.dynamic_slice(jnp.concatenate([low_t, table], axis=1), (0, begin), (D, CAP))
-    own = jnp.where(valid, own, 0.0)
-    own_s = lax.dynamic_slice(jnp.concatenate([low_s, saved_state])[None], (0, begin), (1, CAP))
-    own_s = jnp.where(valid, own_s, 1.0)
-
-    rows8 = jnp.broadcast_to(own_s, (8, CAP))
     rel = relations.T
     end_at = rel.shape[1] // CAP * CAP
     rel_end = jnp.pad(rel[:, end_at:], ((0, 0), (0, end_at + 128 - rel.shape[1])))
-    left, state = train_call(blocks, idx[:, 3], idx, own, rows8, rel, rel_end)
+    left, state = train_call(
+        blocks, idx[:, 3], old_starts, new_starts, idx, saved_rows.T, saved_state[None], rel, rel_end)
     return left.T, state[0]
 
 

time: 142 us -> 129 us (0.908); the launches traced: 139 us -> 128 us
  Pallas kernels: 110 us -> 117 us
  starting transfers between devices: 7.23 us -> 0.76 us
  between operations: 6.23 us -> 0.91 us
  local copies, waits for them, and re-layouts: 13 us -> 8.94 us
  other arithmetic: 2.57 us -> 0.68 us
    ppermute x2 -> x0, starting transfers between devices: 7.14 us -> none  [the longest x1 3.72 us: local(): low_s = lax.ppermute(low_s, BOTH, shift)]
    pallas_call x1, Pallas kernels: 110 us -> 117 us  [train_call(): pl.pallas_call(functools.partial(train_kernel, blocks), out_shape=(jax.Sh...]
    dynamic_slice x4 -> x0, local copies, waits for them, and re-layouts: 4.08 us -> none  [the longest x1 1.38 us: tail_end(): even = old_starts[p] - old_starts[jnp.maximum(p - 1, 0)] - CAP]
    select_n x2 -> x0, other arithmetic: 1.88 us -> none  [the longest x1 1.8 us: local(): own = jnp.where(valid, own, 0.0)]
    unnamed x19 -> x11, local copies, waits for them, and re-layouts: 3.38 us -> 4.01 us
  transfers between devices with their start and end apart: 3 -> 1, of which waited for: 0 -> 0; matrix products, arithmetic and copies ran while one was open for 6% -> 2% of each run, Pallas kernels for 0% -> 0%
where the time goes in v5:
time: 129 us; the launch traced here: 128 us
  Pallas kernels  117 us (91%)
  local copies, waits for them, and re-layouts  8.94 us (7%)
    pallas_call x1, Pallas kernels, train_call(): pl.pallas_call(functools.partial(train_kernel, blocks), out_shape=(jax.Sh...  117 us
    unnamed x11, local copies, waits for them, and re-layouts  4.01 us
  transfers between devices with their start and end apart: 1, of which 0 were waited for; matrix products, arithmetic and copies ran while one was open for 2% of the time, Pallas kernels for 0%

profile of v5, /device:TPU:27, one launch (start us, length us, event | category | flops | bytes accessed | tf_op | source)
XLA Modules:
  0.0 128.1 jit_solution(10040917989751907567)
XLA Ops:
  0.6 0.7 fusion.1
  1.3 0.1 broadcast_in_dim.55
  1.4 0.8 constant_dynamic-slice_fusion.1
  2.3 0.9 constant_dynamic-slice_fusion.3
  3.2 0.9 constant_dynamic-slice_fusion
  4.3 0.2 concatenate.7
  4.4 0.8 collective-permute-start
  5.2 0.1 broadcast_in_dim.49
  5.4 0.9 slice.9
  6.4 0.7 pad.46.rel_end
  7.1 0.2 concatenate.6
  7.2 0.0 collective-permute-done
  7.3 0.0 copy-start
  7.3 0.6 copy.30
  7.9 0.0 copy-done
  7.9 116.8 %train.1 = (f32[400,512]{1,0:T(8,128)}, f32[1,512]{1,0:T(1,128)}) custom-call(s32[4,1024]{1,0:T(4,128)} %bitcast.37, s32[64]{0:T(128)} %old.1, s32[128]{0:T(128)} %new.1, s32[4,8,1024]{2,1,0:T(8,128)} %copy-done, f32[400,1024]{1,0:T(8,128)} %bitcast.41, f32[1,1024]{1,0:T(1,128)} %bitcast.42, f32[400,4131]{1,0:T(8,128)} %bitcast.39, f32[400,128]{1,0:T(8,128)} %pad.46.rel_end), custom_call_target="tpu_custom_call" | custom-call | flops 40000000000 | bytes 10000000 | tf_op jit(solution)/shard_map/train/pallas_call | solution.py:483
  124.8 2.1 %copy.37 = f32[512,400]{0,1:T(8,128)} copy(f32[512,400]{0,1:T(8,128)} %bitcast.32) | data formatting | bytes 1638400
  126.9 1.3 copy.38
  (29 shorter events, 0.3 us)
Async XLA Ops:
  4.4 2.8 %collective-permute-start = (s32[4,8,1024]{2,1,0:T(8,128)S(1)}, s32[4,8,1024]{2,1,0:T(8,128)S(1)}, u32[]{:S(2)}, u32[]{:S(2)}) collective-permute-start(s32[4,8,1024]{2,1,0:T(8,128)S(1)} %concatenate.7), channel_id=1, source_target_pairs={{0,2},{2,0},{1,3},{3,1},{4,6},{6,4},{5,7},{7,5},{8,10},{10,8},{9,1... | collective-permute-start | bytes 393224 | tf_op jit(solution)/shard_map/ppermute | solution.py:554
  7.3 0.7 copy-start

commit v6 on v5

--- a/solution.py
+++ b/solution.py
@@ -212,17 +212,13 @@
     get_rel(full).wait()
     rel_s[full * CAP :, :] = gro[0, :, 0:128].T[0 : rel.shape[1] - full * CAP]
 
-    def gather(s):
-        def body(k, carry):
-            base = pl.multiple_of(k * 128, 128)
-            for i in range(128):
-                rows[i : i + 1, 0:D] = rel_s[pl.ds(ids[s, base + i], 1), :]
-            rel_t[:, pl.ds(base, 128)] = rows[...].T[0:D]
-            return carry
-
-        lax.fori_loop(0, E // 128, body, 0)
-
-    gather(0)
+    def gather_block(s, p, k):
+        for i in range(128):
+            rows[k % 2, i : i + 1, 0:D] = rel_s[pl.ds(ids[s, k * 128 + i], 1), :]
+        rel_t[p, :, k * 128 : (k + 1) * 128] = rows[k % 2].T[0:D]
+
+    for k in range(E // 128):
+        gather_block(0, 0, k)
     share.wait_recv()
     share_state.wait_recv()
 
@@ -267,8 +263,8 @@
             d = dh[0:D] + dh[D : 2 * D]
             s_re = sh[0:H] + sh[D : D + H]
             s_im = sh[H:D] + sh[D + H : 2 * D]
-            r_re = rel_t[0:H, col]
-            r_im = rel_t[H:D, col]
+            r_re = rel_t[p, 0:H, col]
+            r_im = rel_t[p, H:D, col]
             q_s[0:H, :] = s_re * r_re - s_im * r_im
             q_s[H:D, :] = s_re * r_im + s_im * r_re
             q = q_s[...]
@@ -281,6 +277,8 @@
             qb_s[:, col] = qb
             scores = dot(nb, qb, NN)
             dn_s[:, col] = (jax.nn.sigmoid(scores) * (live * (1.0 / N))).astype(BF)
+            for k in range(CH // 128):
+                gather_block(lax.rem(s + 1, STEPS), 1 - p, e * (CH // 128) + k)
         split_to(gdhl, pl.ds(E, N), dot(qb_s[...], dn_s[...], NT))
 
         @pl.when(jnp.logical_and(s == 0, r + c == 0))
@@ -298,8 +296,8 @@
 
         def source_grad(e):
             col = pl.ds(e * CH, CH)
-            r_re = rel_t[0:H, col]
-            r_im = rel_t[H:D, col]
+            r_re = rel_t[p, 0:H, col]
+            r_im = rel_t[p, H:D, col]
             g_s[...] = dp_s[:, col] * d_s[:, col] + dot(nbt, dn_s[:, col], NN)
             g_re = g_s[0:H, :]
             g_im = g_s[H:D, :]
@@ -326,6 +324,30 @@
         def _():
             home_copy(s).start()
 
+        @pl.when(jnp.logical_and(s == 1, r + c == 2))
+        def _():
+            t1.wait_recv()
+            share_on.start()
+
+        @pl.when(jnp.logical_and(s == r + 1, c == 0))
+        def _():
+            t2a.wait_recv()
+
+            @pl.when(r == 0)
+            def _():
+                relay.wait_recv()
+
+            share_on.start()
+
+        @pl.when(jnp.logical_and(s == 0, r > c))
+        def _():
+            t2a.start()
+
+        @pl.when(jnp.logical_and(s == 2, r < c))
+        def _():
+            t3.wait_recv()
+            share_far.start()
+
         for e in range(1, E // CH):
             source_grad(e)
         left_half(theirs)
@@ -336,45 +358,14 @@
         def _():
             gl_copy(s, 1).start()
 
-        @pl.when(jnp.logical_and(s == r, c == 1))
+        @pl.when(jnp.logical_and(s == 0, r < c))
         def _():
             t1.wait_recv()
             share_on.start()
 
-        @pl.when(jnp.logical_and(s == r + 1, c == 0))
-        def _():
-            t2a.wait_recv()
-
-            @pl.when(r == 0)
-            def _():
-                relay.wait_recv()
-
-            share_on.start()
-
-        @pl.when(jnp.logical_and(s == 0, r > c))
-        def _():
-            t2a.start()
-
-        @pl.when(jnp.logical_and(s == 2, r < c))
-        def _():
-            t3.wait_recv()
-            share_far.start()
-
-        @pl.when(s < STEPS - 1)
-        def _():
-            gather(s + 1)
-
         @pl.when(jnp.logical_and(s == 0, r < c))
         def _():
             t3.start()
-
-        @pl.when(s == r + c)
-        def _():
-            share_on.wait_recv()
-
-        @pl.when(jnp.logical_and(s == 2, r + c == 0))
-        def _():
-            share_far.wait_recv()
 
         @pl.when(jnp.logical_and(s == 1, here))
         def _():
@@ -405,6 +396,14 @@
                 state[:, col] = v
                 left[:, col] = x
                 split_to(lhl, col, x)
+
+        @pl.when(s == r + c)
+        def _():
+            share_on.wait_recv()
+
+        @pl.when(jnp.logical_and(s == 2, r + c == 0))
+        def _():
+            share_far.wait_recv()
 
         return carry
 
@@ -491,8 +490,8 @@
             pltpu.VMEM((5, D, CAP), F32),
             pltpu.VMEM((2, 8, CAP), F32),
             pltpu.VMEM(rel.shape[::-1], F32),
-            pltpu.VMEM((D, E), F32),
-            pltpu.VMEM((128, ROWS_W), F32),
+            pltpu.VMEM((2, D, E), F32),
+            pltpu.VMEM((2, 128, ROWS_W), F32),
             pltpu.VMEM((D, CAP), F32),
             pltpu.VMEM((8, CAP), F32),
             pltpu.VMEM((2 * D, CAP), BF),

time: 129 us -> 131 us (1.016)
  Pallas kernels: 117 us -> 119 us
    pallas_call x1, Pallas kernels: 117 us -> 119 us  [train_call(): pl.pallas_call(functools.partial(train_kernel, blocks), out_shape=(jax.Sh...]
where the time goes in v6:
time: 131 us; the launch traced here: 130 us
  Pallas kernels  119 us (91%)
  local copies, waits for them, and re-layouts  8.94 us (7%)
    pallas_call x1, Pallas kernels, train_call(): pl.pallas_call(functools.partial(train_kernel, blocks), out_shape=(jax.Sh...  119 us
    unnamed x11, local copies, waits for them, and re-layouts  4.01 us
  transfers between devices with their start and end apart: 1, of which 0 were waited for; matrix products, arithmetic and copies ran while one was open for 2% of the time, Pallas kernels for 0%

profile of v6, /device:TPU:27, one launch (start us, length us, event | category | flops | bytes accessed | tf_op | source)
XLA Modules:
  0.0 130.3 jit_solution(8180047500403536853)
XLA Ops:
  0.6 0.7 fusion.1
  1.3 0.1 broadcast_in_dim.55
  1.4 0.8 constant_dynamic-slice_fusion.1
  2.3 0.9 constant_dynamic-slice_fusion.3
  3.2 0.9 constant_dynamic-slice_fusion
  4.3 0.2 concatenate.7
  4.4 0.8 collective-permute-start
  5.2 0.1 broadcast_in_dim.49
  5.4 0.9 slice.9
  6.4 0.7 pad.46.rel_end
  7.1 0.2 concatenate.6
  7.2 0.0 collective-permute-done
  7.3 0.0 copy-start
  7.3 0.6 copy.30
  7.9 0.0 copy-done
  7.9 119.0 %train.1 = (f32[400,512]{1,0:T(8,128)}, f32[1,512]{1,0:T(1,128)}) custom-call(s32[4,1024]{1,0:T(4,128)} %bitcast.37, s32[64]{0:T(128)} %old.1, s32[128]{0:T(128)} %new.1, s32[4,8,1024]{2,1,0:T(8,128)} %copy-done, f32[400,1024]{1,0:T(8,128)} %bitcast.41, f32[1,1024]{1,0:T(1,128)} %bitcast.42, f32[400,4131]{1,0:T(8,128)} %bitcast.39, f32[400,128]{1,0:T(8,128)} %pad.46.rel_end), custom_call_target="tpu_custom_call" | custom-call | flops 40000000000 | bytes 10000000 | tf_op jit(solution)/shard_map/train/pallas_call | solution.py:482
  126.9 2.1 %copy.37 = f32[512,400]{0,1:T(8,128)} copy(f32[512,400]{0,1:T(8,128)} %bitcast.32) | data formatting | bytes 1638400
  129.0 1.3 copy.38
  (29 shorter events, 0.3 us)
Async XLA Ops:
  4.4 2.8 %collective-permute-start = (s32[4,8,1024]{2,1,0:T(8,128)S(1)}, s32[4,8,1024]{2,1,0:T(8,128)S(1)}, u32[]{:S(2)}, u32[]{:S(2)}) collective-permute-start(s32[4,8,1024]{2,1,0:T(8,128)S(1)} %concatenate.7), channel_id=1, source_target_pairs={{0,2},{2,0},{1,3},{3,1},{4,6},{6,4},{5,7},{7,5},{8,10},{10,8},{9,1... | collective-permute-start | bytes 393224 | tf_op jit(solution)/shard_map/ppermute | solution.py:553
  7.3 0.7 copy-start

commit v7 on v6

--- a/solution.py
+++ b/solution.py
@@ -281,10 +281,6 @@
                 gather_block(lax.rem(s + 1, STEPS), 1 - p, e * (CH // 128) + k)
         split_to(gdhl, pl.ds(E, N), dot(qb_s[...], dn_s[...], NT))
 
-        @pl.when(jnp.logical_and(s == 0, r + c == 0))
-        def _():
-            t2a.start()
-
         @pl.when(jnp.logical_and(s == 0, r > c))
         def _():
             t2b.wait_recv()
@@ -320,7 +316,7 @@
         def _():
             home_local(s).start()
 
-        @pl.when(jnp.logical_or(s > 0, jnp.logical_not(here)))
+        @pl.when(s > 0)
         def _():
             home_copy(s).start()
 
@@ -353,6 +349,14 @@
         left_half(theirs)
         gl_copy(s, 0).start()
         left_half(mine)
+
+        @pl.when(jnp.logical_and(s == 0, r + c == 0))
+        def _():
+            t2a.start()
+
+        @pl.when(jnp.logical_and(s == 0, jnp.logical_not(here)))
+        def _():
+            home_copy(0).start()
 
         @pl.when(s < STEPS - 1)
         def _():

time: 131 us -> 131 us (level)
  no operation moved by 1% of the time
where the time goes in v7:
time: 131 us; the launch traced here: 130 us
  Pallas kernels  119 us (91%)
  local copies, waits for them, and re-layouts  8.94 us (7%)
    pallas_call x1, Pallas kernels, train_call(): pl.pallas_call(functools.partial(train_kernel, blocks), out_shape=(jax.Sh...  119 us
    unnamed x11, local copies, waits for them, and re-layouts  4.01 us
  transfers between devices with their start and end apart: 1, of which 0 were waited for; matrix products, arithmetic and copies ran while one was open for 2% of the time, Pallas kernels for 0%

profile of v7, /device:TPU:27, one launch (start us, length us, event | category | flops | bytes accessed | tf_op | source)
XLA Modules:
  0.0 130.2 jit_solution(1817429824555603895)
XLA Ops:
  0.6 0.7 fusion.1
  1.3 0.1 broadcast_in_dim.55
  1.4 0.8 constant_dynamic-slice_fusion.1
  2.3 0.9 constant_dynamic-slice_fusion.3
  3.2 0.9 constant_dynamic-slice_fusion
  4.3 0.2 concatenate.7
  4.4 0.8 collective-permute-start
  5.2 0.1 broadcast_in_dim.49
  5.4 0.9 slice.9
  6.4 0.7 pad.46.rel_end
  7.1 0.2 concatenate.6
  7.2 0.0 collective-permute-done
  7.3 0.0 copy-start
  7.3 0.6 copy.30
  7.9 0.0 copy-done
  7.9 118.9 %train.1 = (f32[400,512]{1,0:T(8,128)}, f32[1,512]{1,0:T(1,128)}) custom-call(s32[4,1024]{1,0:T(4,128)} %bitcast.37, s32[64]{0:T(128)} %old.1, s32[128]{0:T(128)} %new.1, s32[4,8,1024]{2,1,0:T(8,128)} %copy-done, f32[400,1024]{1,0:T(8,128)} %bitcast.41, f32[1,1024]{1,0:T(1,128)} %bitcast.42, f32[400,4131]{1,0:T(8,128)} %bitcast.39, f32[400,128]{1,0:T(8,128)} %pad.46.rel_end), custom_call_target="tpu_custom_call" | custom-call | flops 40000000000 | bytes 10000000 | tf_op jit(solution)/shard_map/train/pallas_call | solution.py:486
  126.9 2.1 %copy.37 = f32[512,400]{0,1:T(8,128)} copy(f32[512,400]{0,1:T(8,128)} %bitcast.32) | data formatting | bytes 1638400
  129.0 1.3 copy.38
  (29 shorter events, 0.3 us)
Async XLA Ops:
  4.4 2.8 %collective-permute-start = (s32[4,8,1024]{2,1,0:T(8,128)S(1)}, s32[4,8,1024]{2,1,0:T(8,128)S(1)}, u32[]{:S(2)}, u32[]{:S(2)}) collective-permute-start(s32[4,8,1024]{2,1,0:T(8,128)S(1)} %concatenate.7), channel_id=1, source_target_pairs={{0,2},{2,0},{1,3},{3,1},{4,6},{6,4},{5,7},{7,5},{8,10},{10,8},{9,1... | collective-permute-start | bytes 393224 | tf_op jit(solution)/shard_map/ppermute | solution.py:557
  7.3 0.7 copy-start
